TPU v7x, 32 devices: a whole 2x2x4 slice. The times are simulated.
32 devices in a mesh: rows: 4 (over z), cols: 8 (over y, x, core).
Axes of the slice: x: 2, y: 2, z: 4, core: 2. Of those that a mesh axis runs over, the one named last changes fastest.
Arguments:
- pixels: bfloat16 [3, 512, 2048], P(None, 'rows', 'cols'), may hold values from -6 to 6
- patch_weight: bfloat16 [48, 256], replicated, may hold values from -0.875 to 0.875
- patch_bias: float32 [256], replicated, may hold values from -4 to 4
- conv_kernel: float32 [49, 256], replicated, may hold values from -0.875 to 0.875
- norm_gain: float32 [256], replicated, may hold values from 0.1 to 1.9
- kv_weight: bfloat16 [256, 2048], replicated, may hold values from -0.375 to 0.375
- latents: bfloat16 [256, 1024], replicated, may hold values from -80 to 80, as said below
- d_attended: bfloat16 [256, 1024], replicated, may hold values from -6 to 6
Outputs:
- attended: float32 [256, 1024], replicated
- grad_latents: float32 [256, 1024], replicated
- grad_kv_weight: float32 [256, 2048], replicated
- grad_norm_gain: float32 [256], replicated
- grad_conv_kernel: float32 [49, 256], replicated
- grad_patch_weight: float32 [48, 256], replicated
- grad_patch_bias: float32 [256], replicated
Inputs may be any that keep to these rules, and one draw needn't show every extreme that they name: `latents`: each latent row has its own scale.
All inputs are finite; a program needn't handle non-finite values.
Results may differ from a plain program's by a relative error of at most 0.035.
The roundings to bfloat16 on the way count: a program that leaves them out, or rounds other values in their place, can miss the bound.
Values may be sent and summed in bfloat16 or wider, within the bound.
A program may use at most 576 MiB of HBM per device.

v0:
```python
import jax
import jax.numpy as jnp
from jax import lax
from jax.sharding import PartitionSpec as P

PATCH = 4
KSIZE = 7
HEADS = 8


norm_eps = 1e-05


def padded_2(x, sides, width):
    for axis, dim in sides:
        devices, length = (lax.axis_size(axis), x.shape[dim])
        up = [(i, (i + 1) % devices) for i in range(devices - 1)]
        down = [(j, i) for i, j in up]
        last = lax.slice_in_dim(x, length - width, length, axis=dim)
        leading = lax.slice_in_dim(x, 0, width, axis=dim)
        before = lax.ppermute(last, axis, up)
        after = lax.ppermute(leading, axis, down)
        x = jnp.concatenate([before, x, after], axis=dim)
    return x


def patch_rows(pixels):
    in_channels, height, image_width = pixels.shape
    blocks = pixels.reshape(in_channels, height // PATCH, PATCH, image_width // PATCH, PATCH)
    blocks = blocks.transpose(1, 3, 0, 2, 4)
    return blocks.reshape(height // PATCH * (image_width // PATCH), in_channels * PATCH * PATCH)


def depthwise(padded, kernel, tile_rows, tile_cols):
    result = jnp.zeros((tile_rows, tile_cols, kernel.shape[1]), jnp.float32)
    for offset_row in range(KSIZE):
        for offset_col in range(KSIZE):
            window = padded[
                offset_row : offset_row + tile_rows, offset_col : offset_col + tile_cols
            ].astype(jnp.float32)
            result = result + window * kernel[offset_row * KSIZE + offset_col]
    return result


def transposed(padded, kernel, tile_rows, tile_cols):
    result = jnp.zeros((tile_rows, tile_cols, kernel.shape[1]), jnp.float32)
    last = KSIZE - 1
    for offset_row in range(KSIZE):
        for offset_col in range(KSIZE):
            start_row = last - offset_row
            start_col = last - offset_col
            window = padded[
                start_row : start_row + tile_rows, start_col : start_col + tile_cols
            ].astype(jnp.float32)
            result = result + window * kernel[offset_row * KSIZE + offset_col]
    return result


def kernel_grad(padded, upstream, tile_rows, tile_cols):
    upstream_f = upstream.astype(jnp.float32)
    kernel_terms = []
    for offset_row in range(KSIZE):
        for offset_col in range(KSIZE):
            window = padded[
                offset_row : offset_row + tile_rows, offset_col : offset_col + tile_cols
            ].astype(jnp.float32)
            kernel_terms.append(jnp.sum(window * upstream_f, axis=(0, 1)))
    return jnp.stack(kernel_terms)


def normalize(mixed):
    centre = mixed - jnp.mean(mixed, axis=-1, keepdims=True)
    variance = jnp.mean(centre * centre, axis=-1, keepdims=True)
    inverse = lax.rsqrt(variance + norm_eps)
    return (centre * inverse, inverse)


def split_heads(matrix, head_count):
    return matrix.reshape(matrix.shape[0], head_count, -1).transpose(1, 0, 2)


def merge_heads(stacked):
    return stacked.transpose(1, 0, 2).reshape(stacked.shape[1], -1)


def head_state(pieces):
    queries, key_rows, values = pieces
    score_scale = queries.shape[-1] ** (-0.5)
    scores = (
        jnp.einsum("le,te->lt", queries, key_rows, preferred_element_type=jnp.float32) * score_scale
    )
    top_score = jnp.max(scores, axis=1)
    raised = jnp.exp(scores - top_score[:, None])
    weighted = jnp.dot(raised.astype(jnp.bfloat16), values, preferred_element_type=jnp.float32)
    return (top_score, jnp.sum(raised, axis=1), weighted)


def head_grads(pieces):
    queries, key_rows, values, top_score, sum_exp, row_dots, upstream = pieces
    score_scale = queries.shape[-1] ** (-0.5)
    scores = (
        jnp.einsum("le,te->lt", queries, key_rows, preferred_element_type=jnp.float32) * score_scale
    )
    probs = jnp.exp(scores - top_score[:, None]) / sum_exp[:, None]
    d_probs = jnp.einsum("le,te->lt", upstream, values, preferred_element_type=jnp.float32)
    d_scores = (probs * (d_probs - row_dots[:, None]) * score_scale).astype(jnp.bfloat16)
    q_grad = jnp.einsum("lt,te->le", d_scores, key_rows, preferred_element_type=jnp.float32)
    k_grad = jnp.einsum("lt,le->te", d_scores, queries, preferred_element_type=jnp.float32).astype(
        jnp.bfloat16
    )
    v_grad = jnp.einsum(
        "lt,le->te", probs.astype(jnp.bfloat16), upstream, preferred_element_type=jnp.float32
    )
    return (q_grad, k_grad, v_grad.astype(jnp.bfloat16))


def rescaled(local_top, local_sum, local_weighted, top_score):
    factor = jnp.exp(local_top - top_score)
    latent_count, head_count = factor.shape
    weighted = local_weighted.reshape(latent_count, head_count, -1) * factor[:, :, None]
    return (local_sum * factor, weighted.reshape(latent_count, -1))


def normalized(weighted, sum_exp):
    latent_count, head_count = sum_exp.shape
    return (weighted.reshape(latent_count, head_count, -1) / sum_exp[:, :, None]).reshape(
        latent_count, -1
    )


def per_device(
    pixels, patch_weight, patch_bias, conv_kernel, norm_gain, kv_weight, latents, d_attended
):
    tile_rows = pixels.shape[1] // PATCH
    tile_cols = pixels.shape[2] // PATCH
    channels = patch_weight.shape[1]
    model_dim = latents.shape[1]
    latent_count = latents.shape[0]
    patches = patch_rows(pixels)
    embedded = (
        jnp.dot(patches, patch_weight, preferred_element_type=jnp.float32) + patch_bias
    ).astype(jnp.bfloat16)
    embedded = embedded.reshape(tile_rows, tile_cols, channels)
    padded = padded_2(embedded, (("rows", 0), ("cols", 1)), KSIZE // 2)
    mixed = embedded.astype(jnp.float32) + depthwise(padded, conv_kernel, tile_rows, tile_cols)
    centred, inverse = normalize(mixed)
    normed = (centred * norm_gain).astype(jnp.bfloat16).reshape(tile_rows * tile_cols, channels)
    projected = jnp.dot(normed, kv_weight, preferred_element_type=jnp.float32).astype(jnp.bfloat16)
    query_heads = split_heads(latents, HEADS)
    key_heads = split_heads(projected[:, :model_dim], HEADS)
    value_heads = split_heads(projected[:, model_dim:], HEADS)
    tops, sums, weighteds = lax.map(head_state, (query_heads, key_heads, value_heads))
    local_top = tops.T
    local_sum = sums.T
    local_weighted = merge_heads(weighteds)
    top_score = lax.pmax(local_top, ("rows", "cols"))
    part_sum, part_weighted = rescaled(local_top, local_sum, local_weighted, top_score)
    sum_exp, weighted = lax.psum((part_sum, part_weighted), ("rows", "cols"))
    attended = normalized(weighted, sum_exp)
    row_dots = jnp.sum(
        d_attended.astype(jnp.float32).reshape(latent_count, HEADS, -1)
        * attended.reshape(latent_count, HEADS, -1),
        axis=2,
    )
    q_grads, k_grads, v_grads = lax.map(
        head_grads,
        (
            query_heads,
            key_heads,
            value_heads,
            top_score.T,
            sum_exp.T,
            row_dots.T,
            split_heads(d_attended, HEADS),
        ),
    )
    local_latents = merge_heads(q_grads)
    d_projected = jnp.concatenate([merge_heads(k_grads), merge_heads(v_grads)], axis=1)
    local_kv = jnp.einsum("tc,tk->ck", normed, d_projected, preferred_element_type=jnp.float32)
    d_normed = jnp.einsum("tk,ck->tc", d_projected, kv_weight, preferred_element_type=jnp.float32)
    d_normed = d_normed.reshape(tile_rows, tile_cols, channels)
    local_gain = jnp.sum(d_normed * centred, axis=(0, 1))
    scaled = d_normed * norm_gain
    d_mixed = inverse * (
        scaled
        - jnp.mean(scaled, axis=-1, keepdims=True)
        - centred * jnp.mean(scaled * centred, axis=-1, keepdims=True)
    )
    d_mixed = d_mixed.astype(jnp.bfloat16)
    local_kernel = kernel_grad(padded, d_mixed, tile_rows, tile_cols)
    d_padded = padded_2(d_mixed, (("rows", 0), ("cols", 1)), KSIZE // 2)
    d_embedded = (
        d_mixed.astype(jnp.float32) + transposed(d_padded, conv_kernel, tile_rows, tile_cols)
    ).astype(jnp.bfloat16)
    d_embedded = d_embedded.reshape(tile_rows * tile_cols, channels)
    local_patch = jnp.einsum("tp,tc->pc", patches, d_embedded, preferred_element_type=jnp.float32)
    local_bias = jnp.sum(d_embedded.astype(jnp.float32), axis=0)
    grad_latents, grad_kv, grad_gain, grad_kernel, grad_patch, grad_bias = lax.psum(
        (local_latents, local_kv, local_gain, local_kernel, local_patch, local_bias),
        ("rows", "cols"),
    )
    return (attended, grad_latents, grad_kv, grad_gain, grad_kernel, grad_patch, grad_bias)


def solution(mesh):
    return jax.shard_map(
        per_device,
        mesh=mesh,
        in_specs=(P(None, "rows", "cols"), P(), P(), P(), P(), P(), P(), P()),
        out_specs=(P(), P(), P(), P(), P(), P(), P()),
        check_vma=False,
    )
```

profile of v0, /device:TPU:0, one launch (start us, length us, event | category | flops | bytes accessed | tf_op | source)
XLA Modules:
  0.0 803.1 jit_solution(8520691981970709505)
XLA Ops:
  7.2 15.3 %reshape.154 = bf16[3,32,4,64,4]{4,3,2,1,0:T(8,128)(2,1)} reshape(bf16[3,128,256]{2,1,0:T(8,128)(2,1)} %param.12) | data formatting | bytes 393216 | tf_op jit(solution)/shard_map/reshape | solution.py:29
  22.6 6.0 copy.22
  30.8 5.6 collective-permute-start
  47.5 19.2 %fusion.180 = (f32[32,64]{1,0:T(8,128)S(1)}, f32[32,64,256]{2,1,0:T(8,128)S(1)}) fusion(f32[256]{0:T(256)} %bitcast.382, bf16[38,67,256]{2,1,0:T(8,128)(2,1)S(1)} %get-tuple-element.249, f32[256]{0:T(256)} %bitcast.384, f32[256]{0:T(256)S(1)} %bitcast.290, f32[256]{0:T(256)S(1)} %bitcast.292, bf16[3,64,256]{2,1,0:T(8,128)(2,1)S(1)} %copy-done.16, ...), kind=kLoop, calls=%fused_computation.344 | loop fusion | flops 80738304 | bytes 47440896 | tf_op jit(solution)/shard_map/reduce_sum | solution.py:72
  68.1 2.4 convolution_convert_fusion.2
  70.5 3.6 fusion.182
  74.2 6.4 copy.24
  80.6 6.4 copy.23
  87.1 39.8 %while.28 = (s32[]{:T(128)}, f32[8,256]{1,0:T(8,128)S(1)}, f32[8,256]{1,0:T(8,128)}, f32[8,256,128]{2,1,0:T(8,128)S(1)}, bf16[8,256,128]{2,1,0:T(8,128)(2,1)}, /...) while((s32[]{:T(128)}, f32[8,256]{1,0:T(8,128)S(1)}, ...), condition=%wide.region_5.6_spmd, body=%wide.region_2.5_spmd.sunk | while | flops 271580672 | bytes 7546989 | solution.py:152
  127.5 44.0 %pmax.7 = f32[256,8]{0,1:T(8,128)S(1)} all-reduce(f32[256,8]{0,1:T(8,128)} %bitcast.284), channel_id=1, replica_groups=mesh['rows'=4,'cols'=8] {'rows','cols'}, use_global_device_ids=true, to_apply=%region_6.7 | all-reduce | flops 2048 | bytes 16384 | tf_op jit(solution)/shard_map/pmax | solution.py:156
  176.3 41.5 %psum.57 = f32[256,8]{0,1:T(8,128)S(1)} all-reduce(f32[256,8]{0,1:T(8,128)S(1)} %copy-done.32), channel_id=1, replica_groups=mesh['rows'=4,'cols'=8] {'rows','cols'}, use_global_device_ids=true, to_apply=%region_8.9 | all-reduce | flops 2048 | bytes 16384 | tf_op jit(solution)/shard_map/psum | solution.py:158
  217.8 87.3 %all-reduce.6.cloned.1.call-done = f32[256,1024]{1,0:T(8,128)} async-done(((f32[256,1024]{1,0:T(8,128)}), f32[256,1024]{1,0:T(8,128)}) %all-reduce.6.cloned.1.call-update) | async-done | bytes 1048592 | tf_op jit(solution)/shard_map/psum | solution.py:158
  309.6 126.1 %while.29 = (s32[]{:T(128)}, f32[8,256,128]{2,1,0:T(8,128)}, bf16[8,2048,128]{1,2,0:T(8,128)(2,1)}, bf16[8,2048,128]{1,2,0:T(8,128)(2,1)}, bf16[8,256,128]{2,1,0...) while((s32[]{:T(128)}, f32[8,256,128]{2,1,0:T(8,128)}, ...), condition=%wide.region_11.12_spmd, body=%wide.region_10.11_spmd.sunk | while | flops 675807232 | bytes 16658581 | solution.py:165
  311.9 2.1 fusion.238
  319.9 2.1 fusion.237
  323.2 2.1 constant_dynamic-update-slice_fusion.3
  327.7 2.1 fusion.238
  333.5 2.1 fusion.239
  335.7 2.1 fusion.237
  339.0 2.2 constant_dynamic-update-slice_fusion.3
  343.6 2.1 fusion.238
  349.3 2.1 fusion.239
  351.5 2.1 fusion.237
  359.3 2.1 fusion.238
  365.1 2.1 fusion.239
  375.0 2.1 fusion.238
  380.8 2.1 fusion.239
  383.0 2.1 fusion.237
  390.8 2.1 fusion.238
  398.7 2.1 fusion.237
  406.6 2.1 fusion.238
  412.4 2.1 fusion.239
  414.5 2.1 fusion.237
  422.3 2.1 fusion.238
  430.2 2.1 fusion.237
  435.7 7.3 multiply_reduce_fusion.1
  443.7 4.5 multiply_reduce_fusion
  448.2 6.6 fusion.137
  454.9 6.5 fusion.141
  461.3 3.3 collective-permute-start.4
  466.6 5.6 fusion.140
  472.2 8.2 %fusion.43 = f32[256,2048]{1,0:T(8,128)} fusion(bf16[2048,256]{1,0:T(8,128)(2,1)S(1)} %bitcast.272, bf16[2048,1024]{0,1:T(8,128)(2,1)S(1)} %bitcast.436, bf16[2048,1024]{0,1:T(8,128)(2,1)S(1)} %bitcast.438), kind=kOutput, calls=%fused_computation.108 | convolution fusion | flops 2164260864 | bytes 11534336 | tf_op jit(solution)/shard_map/tc,tk->ck/dot_general | solution.py:179
  482.6 3.7 collective-permute-start.7
  487.8 9.1 %stack.199 = f32[49,256]{1,0:T(8,128)} concatenate(f32[1,256]{1,0:T(1,128)} %bitcast.434, f32[1,256]{1,0:T(1,128)} %bitcast.433, f32[1,256]{1,0:T(1,128)} %bitcast.432, f32[1,256]{1,0:T(1,128)} %bitcast.428, f32[1,256]{1,0:T(1,128)} %bitcast.424, f32[1,256]{1,0:T(1,128)} %bitcast.423, f32[1,256]{1,0:T(1,128)} %bitcast.405, f32[1,256]{1,0:T(1,128)S(1)} %bitcast.387, ...), dimensions={0} | concatenate | bytes 100352 | tf_op jit(solution)/shard_map/stack | solution.py:68
  499.4 21.4 %convert_reduce_fusion = (f32[256]{0:T(256)}, bf16[32,64,256]{2,1,0:T(8,128)(2,1)S(1)}) fusion(f32[256]{0:T(256)} %bitcast.383, bf16[38,67,256]{2,1,0:T(8,128)(2,1)S(1)} %get-tuple-element.245, f32[256]{0:T(256)} %bitcast.385, f32[256]{0:T(256)S(1)} %bitcast.291, f32[256]{0:T(256)S(1)} %bitcast.293, bf16[32,64,256]{2,1,0:T(8,128)(2,1)S(1)} %get-tuple-element.233, ...), kind=kLoop, calls=%fused_computation.283 | loop fusion | flops 81788672 | bytes 46385152 | tf_op jit(solution)/shard_map/reduce_sum | solution.py:197
  527.0 117.2 %all-reduce.8.cloned.1.call-done = (f32[256]{0:T(256)}, f32[49,256]{1,0:T(8,128)}, f32[48,256]{1,0:T(8,128)}, f32[256]{0:T(256)}) async-done(((f32[256]{0:T(256)}, f32[49,256]{1,0:T(8,128)}, f32[48,256]{1,0:T(8,128)}, f32[256]{0:T(256)}), (f32[256]{0:T(256)}, f32[49,256]{1,0:T(8,128)}, f32[48,256]{1,0:T(8,128)}, f32[256]{0:T(256)})) %all-reduce.8.cloned.1.call-update) | async-done | bytes 101392 | tf_op jit(solution)/shard_map/psum | solution.py:198
  644.2 146.2 %all-reduce.10.cloned.1.call-done = (f32[256,1024]{1,0:T(8,128)}, f32[256,2048]{1,0:T(8,128)}) async-done(((f32[256,1024]{1,0:T(8,128)}, f32[256,2048]{1,0:T(8,128)}), (f32[256,1024]{1,0:T(8,128)}, f32[256,2048]{1,0:T(8,128)})) %all-reduce.10.cloned.1.call-update) | async-done | bytes 3145744 | tf_op jit(solution)/shard_map/psum | solution.py:198
  790.4 2.5 copy.87
  (415 shorter events, 160.2 us)
Async XLA Ops:
  7.2 61.0 %copy-start = (bf16[256,2048]{1,0:T(8,128)(2,1)S(1)}, bf16[256,2048]{1,0:T(8,128)(2,1)}, u32[]{:S(2)}) copy-start(bf16[256,2048]{1,0:T(8,128)(2,1)} %param.17) | copy-start | bytes 3145732
  7.2 298.0 %all-reduce.6.cloned.1.call-start = ((), (), s32[]{:S(2)}) async-start(), calls=%async_computation | async-start | bytes 2097152 | tf_op jit(solution)/shard_map/psum | solution.py:158
  22.6 6.4 copy-start.33
  22.6 6.4 copy-start.121
  28.6 7.8 copy-start.30
  28.6 13.5 %copy-start.25 = (bf16[256,1024]{1,0:T(8,128)(2,1)S(1)}, bf16[256,1024]{1,0:T(8,128)(2,1)}, u32[]{:S(2)}) copy-start(bf16[256,1024]{1,0:T(8,128)(2,1)} %param.18) | copy-start | bytes 1572868
  29.0 13.1 %copy-start.13 = (bf16[2048,48]{0,1:T(8,128)(2,1)}, bf16[2048,48]{0,1:T(8,128)(2,1)S(1)}, u32[]{:S(2)}) copy-start(bf16[2048,48]{0,1:T(8,128)(2,1)S(1)} %reshape.155) | copy-start | bytes 589828
  29.5 17.6 %copy-start.5 = (bf16[2048,256]{1,0:T(8,128)(2,1)}, bf16[2048,256]{1,0:T(8,128)(2,1)S(1)}, u32[]{:S(2)}) copy-start(bf16[2048,256]{1,0:T(8,128)(2,1)S(1)} %fusion.44) | copy-start | bytes 3145732
  29.5 8.2 %collective-permute-start.1 = (bf16[3,64,256]{2,1,0:T(8,128)(2,1)S(1)}, bf16[3,64,256]{2,1,0:T(8,128)(2,1)S(1)}, u32[]{:S(2)}, u32[]{:S(2)}) collective-permute-start(bf16[3,64,256]{2,1,0:T(8,128)(2,1)S(1)} %bitcast.282), channel_id=1, source_target_pairs={{8,0},{16,8},{24,16},{9,1},{17,9},{25,17},{10,2},{18,10},{26,18},{... | collective-permute-start | bytes 294920 | tf_op jit(solution)/shard_map/ppermute | solution.py:22
  30.8 7.8 collective-permute-start
  37.7 4.3 copy-start.15
  38.6 5.0 collective-permute-start.2
  39.9 5.5 collective-permute-start.3
  43.3 3.8 copy-start.37
  43.3 3.8 copy-start.39
  43.3 3.8 copy-start.41
  43.3 3.8 copy-start.43
  43.4 3.8 copy-start.45
  47.1 19.6 %copy-start.1 = (bf16[38,67,256]{2,1,0:T(8,128)(2,1)}, bf16[38,67,256]{2,1,0:T(8,128)(2,1)S(1)}, u32[]{:S(2)}) copy-start(bf16[38,67,256]{2,1,0:T(8,128)(2,1)S(1)} %get-tuple-element.249) | copy-start | bytes 3910660
  174.2 470.0 %all-reduce.8.cloned.1.call-start = ((), (), s32[]{:S(2)}) async-start(), calls=%async_computation.1 | async-start | bytes 217088 | tf_op jit(solution)/shard_map/psum | solution.py:198
  435.7 8.0 copy-start.109
  443.7 4.5 copy-start.4
  443.7 4.5 copy-start.7
  443.7 4.5 copy-start.27
  448.2 6.6 copy-start.2
  454.8 11.7 %copy-start.6 = (bf16[2048,256]{1,0:T(8,128)(2,1)S(1)}, bf16[2048,256]{1,0:T(8,128)(2,1)}, u32[]{:S(2)}) copy-start(bf16[2048,256]{1,0:T(8,128)(2,1)} %copy-done.5) | copy-start | bytes 3145732
  454.8 11.7 %copy-start.17 = (bf16[3,64,256]{2,1,0:T(8,128)(2,1)S(1)}, bf16[3,64,256]{2,1,0:T(8,128)(2,1)}, u32[]{:S(2)}) copy-start(bf16[3,64,256]{2,1,0:T(8,128)(2,1)} %copy-done.15) | copy-start | bytes 294916
  454.8 11.7 %copy-start.20 = (bf16[3,64,256]{2,1,0:T(8,128)(2,1)S(1)}, bf16[3,64,256]{2,1,0:T(8,128)(2,1)}, u32[]{:S(2)}) copy-start(bf16[3,64,256]{2,1,0:T(8,128)(2,1)} %copy-done.18) | copy-start | bytes 294916
  454.8 17.3 %copy-start.123 = (bf16[8,2048,128]{1,2,0:T(8,128)(2,1)S(1)}, bf16[8,2048,128]{1,2,0:T(8,128)(2,1)}, u32[]{:S(2)}) copy-start(bf16[8,2048,128]{1,2,0:T(8,128)(2,1)} %get-tuple-element.109) | copy-start | bytes 12582916
  461.3 19.1 %collective-permute-start.4 = (bf16[3,64,256]{2,1,0:T(8,128)(2,1)S(1)}, bf16[3,64,256]{2,1,0:T(8,128)(2,1)S(1)}, u32[]{:S(2)}, u32[]{:S(2)}) collective-permute-start(bf16[3,64,256]{2,1,0:T(8,128)(2,1)S(1)} %get-tuple-element.252), channel_id=1, source_target_pairs={{0,8},{8,16},{16,24},{1,9},{9,17},{17,25},{2,10},{10,18},{18,26},{... | collective-permute-start | bytes 294920 | tf_op jit(solution)/shard_map/ppermute | solution.py:21
  464.7 7.5 copy-start.9
  464.7 7.5 copy-start.122
  464.7 15.7 %collective-permute-start.5 = (bf16[3,64,256]{2,1,0:T(8,128)(2,1)S(1)}, bf16[3,64,256]{2,1,0:T(8,128)(2,1)S(1)}, u32[]{:S(2)}, u32[]{:S(2)}) collective-permute-start(bf16[3,64,256]{2,1,0:T(8,128)(2,1)S(1)} %get-tuple-element.253), channel_id=1, source_target_pairs={{8,0},{16,8},{24,16},{9,1},{17,9},{25,17},{10,2},{18,10},{26,18},{... | collective-permute-start | bytes 294920 | tf_op jit(solution)/shard_map/ppermute | solution.py:22
  480.4 7.3 copy-start.21
  480.4 7.3 copy-start.23
  481.2 16.1 %collective-permute-start.6 = (bf16[38,3,256]{2,1,0:T(4,128)(2,1)}, bf16[38,3,256]{2,1,0:T(4,128)(2,1)}, u32[]{:S(2)}, u32[]{:S(2)}) collective-permute-start(bf16[38,3,256]{2,1,0:T(4,128)(2,1)} %get-tuple-element.246), channel_id=1, source_target_pairs={{1,0},{2,1},{3,2},{4,3},{5,4},{6,5},{7,6},{9,8},{10,9},{11,10},{12... | collective-permute-start | bytes 175112 | tf_op jit(solution)/shard_map/ppermute | solution.py:22
  482.5 5.3 copy-start.110
  482.5 5.3 copy-start.111
  482.5 5.3 copy-start.112
  482.5 5.3 copy-start.113
  482.5 5.3 copy-start.114
  482.5 5.3 copy-start.115
  482.5 5.3 copy-start.116
  482.6 5.3 copy-start.117
  482.6 5.3 copy-start.118
  482.6 14.8 %collective-permute-start.7 = (bf16[38,3,256]{2,1,0:T(4,128)(2,1)}, bf16[38,3,256]{2,1,0:T(4,128)(2,1)}, u32[]{:S(2)}, u32[]{:S(2)}) collective-permute-start(bf16[38,3,256]{2,1,0:T(4,128)(2,1)} %get-tuple-element.247), channel_id=1, source_target_pairs={{0,1},{1,2},{2,3},{3,4},{4,5},{5,6},{6,7},{8,9},{9,10},{10,11},{11... | collective-permute-start | bytes 175112 | tf_op jit(solution)/shard_map/ppermute | solution.py:21
  499.4 21.4 %copy-start.14 = (bf16[2048,48]{0,1:T(8,128)(2,1)S(1)}, bf16[2048,48]{0,1:T(8,128)(2,1)}, u32[]{:S(2)}) copy-start(bf16[2048,48]{0,1:T(8,128)(2,1)} %copy-done.13) | copy-start | bytes 589828
  521.8 268.6 %all-reduce.10.cloned.1.call-start = ((), (), s32[]{:S(2)}) async-start(), calls=%async_computation.2 | async-start | bytes 6291456 | tf_op jit(solution)/shard_map/psum | solution.py:198
  (87 other events, 238.7 us)
Sparse Core Ops, SparseCore 0:
  174.3 130.7 all-reduce.5
  521.9 122.1 all-reduce.7
  651.4 138.9 all-reduce.9
where the time goes:
time: 808 us; the launch traced here: 803 us
  waiting for transfers between devices  353 us (44%)
  local copies, waits for them, and re-layouts  128 us (16%)
  matrix products  122 us (15%)
  blocking collectives  85.5 us (11%)
  other arithmetic  79.9 us (10%)
  starting transfers between devices  19.8 us (2%)
  between operations  15.6 us (2%)
    psum x2, waiting for transfers between devices, per_device(): lax.psum((local_latents, local_kv, local_gain, local_kernel, local_patch,...  263 us
    psum x1, waiting for transfers between devices, per_device(): sum_exp, weighted = lax.psum((part_sum, part_weighted), ('rows', 'cols'))  87.3 us
    pmax x1, blocking collectives, per_device(): top_score = lax.pmax(local_top, ('rows', 'cols'))  44 us
    dynamic_update_slice x24, local copies, waits for them, and re-layouts, per_device(): lax.map(head_grads, (query_heads, key_heads, value_heads, top_score.T, su...  43.4 us
    psum x1, blocking collectives, per_device(): sum_exp, weighted = lax.psum((part_sum, part_weighted), ('rows', 'cols'))  41.5 us
    reduce_sum x1, other arithmetic, per_device(): local_bias = jnp.sum(d_embedded.astype(jnp.float32), axis=0)  21.4 us
    reduce_sum x4, other arithmetic, kernel_grad(): kernel_terms.append(jnp.sum(window * upstream_f, axis=(0, 1)))  20.2 us
    reduce_sum x1, other arithmetic, normalize(): centre = mixed - jnp.mean(mixed, axis=-1, keepdims=True)  19.2 us
  transfers between devices with their start and end apart: 11, of which 5 were waited for; matrix products, arithmetic and copies ran while one was open for 4% of the time, Pallas kernels for 0%

commit v1 on v0

v1 whole, which is shorter than its diff:
```python
import functools

import jax
import jax.numpy as jnp
from jax import lax
from jax.experimental import pallas as pl
from jax.experimental.pallas import tpu as pltpu
from jax.sharding import PartitionSpec as P

PATCH = 4
KSIZE = 7
HEADS = 8
HALF = KSIZE // 2
LANES = 128
GROUP = 8
LOG2E = 1.4426950408889634
VMEM_LIMIT = 56 * 1024 * 1024

norm_eps = 1e-05
f32 = jnp.float32
bf16 = jnp.bfloat16


def padded_2(x, sides, width):
    for axis, dim in sides:
        devices, length = (lax.axis_size(axis), x.shape[dim])
        up = [(i, (i + 1) % devices) for i in range(devices - 1)]
        down = [(j, i) for i, j in up]
        last = lax.slice_in_dim(x, length - width, length, axis=dim)
        leading = lax.slice_in_dim(x, 0, width, axis=dim)
        before = lax.ppermute(last, axis, up)
        after = lax.ppermute(leading, axis, down)
        x = jnp.concatenate([before, x, after], axis=dim)
    return x


def patch_rows(pixels):
    in_channels, height, image_width = pixels.shape
    blocks = pixels.reshape(in_channels, height // PATCH, PATCH, image_width // PATCH, PATCH)
    blocks = blocks.transpose(1, 3, 0, 2, 4)
    return blocks.reshape(height // PATCH * (image_width // PATCH), in_channels * PATCH * PATCH)


def halves(x):
    rows, cols, channels = x.shape
    return x.reshape(rows, cols, channels // LANES, LANES).transpose(2, 0, 1, 3)


def conv_windows(x_ref, w_ref, out_ref, tile_rows, tile_cols, flipped):
    groups = tile_rows // GROUP

    def body(n, carry):
        h = n // groups
        r0 = (n % groups) * GROUP
        for cb in range(tile_cols // 8):
            acc = x_ref[h, pl.ds(r0 + HALF, GROUP), cb * 8 + HALF : cb * 8 + HALF + 8, :].astype(f32)
            for j in range(KSIZE):
                x = x_ref[h, pl.ds(r0, GROUP + KSIZE - 1), cb * 8 + j : cb * 8 + j + 8, :].astype(f32)
                for i in range(KSIZE):
                    tap = i * KSIZE + j
                    if flipped:
                        tap = KSIZE * KSIZE - 1 - tap
                    acc = acc + x[i : i + GROUP] * w_ref[h, tap][None]
            out_ref[h, pl.ds(r0, GROUP), cb * 8 : cb * 8 + 8, :] = acc
        return carry

    lax.fori_loop(0, 2 * groups, body, 0)


def norm_rows(m0, m1):
    channels = 2 * LANES
    mean = (jnp.sum(m0, axis=-1, keepdims=True) + jnp.sum(m1, axis=-1, keepdims=True)) / channels
    c0 = m0 - mean
    c1 = m1 - mean
    variance = (
        jnp.sum(c0 * c0, axis=-1, keepdims=True) + jnp.sum(c1 * c1, axis=-1, keepdims=True)
    ) / channels
    inverse = lax.rsqrt(variance + norm_eps)
    return c0 * inverse, c1 * inverse, inverse


def forward_kernel(
    tile_rows, tile_cols, x_ref, w_ref, gain_ref, kv_ref, qt_ref, dat_ref,
    mixed_ref, proj_ref, stats_ref, weighted_ref, normed, scores,
):
    tokens = tile_rows * tile_cols

    @pl.when(pl.program_id(0) == 0)
    def _():
        conv_windows(x_ref, w_ref, mixed_ref, tile_rows, tile_cols, False)

        def body(a, carry):
            c0, c1, _ = norm_rows(mixed_ref[0, a], mixed_ref[1, a])
            rows = pl.ds(pl.multiple_of(a * tile_cols, tile_cols), tile_cols)
            normed[rows, :LANES] = (c0 * gain_ref[:, :LANES]).astype(bf16)
            normed[rows, LANES:] = (c1 * gain_ref[:, LANES:]).astype(bf16)
            return carry

        lax.fori_loop(0, tile_rows, body, 0)

    chunk = 512
    scale = LOG2E * LANES**-0.5
    peak = jnp.full((1, scores.shape[1]), -jnp.inf, f32)
    for n in range(tokens // chunk):
        rows = slice(n * chunk, (n + 1) * chunk)
        proj = jnp.dot(normed[rows, :], kv_ref[0], preferred_element_type=f32).astype(bf16)
        proj_ref[0, rows, :] = proj
        s = jnp.dot(proj[:, :LANES], qt_ref[0], preferred_element_type=f32) * scale
        scores[rows, :] = s
        peak = jnp.maximum(peak, jnp.max(s, axis=0, keepdims=True))
    total = jnp.zeros_like(peak)
    weighted = jnp.zeros((LANES, scores.shape[1]), f32)
    for n in range(tokens // chunk):
        rows = slice(n * chunk, (n + 1) * chunk)
        raised = jnp.exp2(scores[rows, :] - peak)
        total = total + jnp.sum(raised, axis=0, keepdims=True)
        weighted = weighted + lax.dot_general(
            proj_ref[0, rows, LANES:], raised.astype(bf16), (((0,), (0,)), ((), ())),
            preferred_element_type=f32,
        )
    stats_ref[0, 0] = peak
    stats_ref[1, 0] = total
    stats_ref[2, 0] = jnp.sum(weighted * dat_ref[0].astype(f32), axis=0, keepdims=True)
    weighted_ref[0] = weighted


def backward_kernel(
    tile_rows, tile_cols, mixed_ref, gain_ref, proj_ref, qt_ref, q_ref, dat_ref, da_ref,
    kvt_ref, shift_ref, dots_ref, top_ref, weighted_ref,
    large_ref, d_mixed_ref, grad_gain_ref, normed, d_proj, d_normed,
):
    tokens = tile_rows * tile_cols
    chunk = 512
    scale = LANES**-0.5

    @pl.when(pl.program_id(0) == 0)
    def _():
        def body(a, carry):
            c0, c1, _ = norm_rows(mixed_ref[0, a], mixed_ref[1, a])
            rows = pl.ds(pl.multiple_of(a * tile_cols, tile_cols), tile_cols)
            normed[rows, :LANES] = (c0 * gain_ref[:, :LANES]).astype(bf16)
            normed[rows, LANES:] = (c1 * gain_ref[:, LANES:]).astype(bf16)
            d_normed[rows, :] = jnp.zeros((tile_cols, 2 * LANES), f32)
            return carry

        lax.fori_loop(0, tile_rows, body, 0)

    shift = shift_ref[0]
    dots = dots_ref[0]
    grad_q = jnp.zeros((LANES, shift.shape[1]), f32)
    grad_kv = jnp.zeros((2 * LANES, 2 * LANES), f32)
    for n in range(tokens // chunk):
        rows = slice(n * chunk, (n + 1) * chunk)
        keys = proj_ref[0, rows, :LANES]
        values = proj_ref[0, rows, LANES:]
        s = jnp.dot(keys, qt_ref[0], preferred_element_type=f32) * (LOG2E * scale)
        probs = jnp.exp2(s - shift)
        d_probs = jnp.dot(values, dat_ref[0], preferred_element_type=f32)
        d_scores = (probs * (d_probs - dots)).astype(bf16)
        grad_q = grad_q + lax.dot_general(
            keys, d_scores, (((0,), (0,)), ((), ())), preferred_element_type=f32
        )
        d_keys = jnp.dot(d_scores, q_ref[0], preferred_element_type=f32) * scale
        d_values = jnp.dot(probs.astype(bf16), da_ref[0], preferred_element_type=f32)
        both = jnp.concatenate([d_keys.astype(bf16), d_values.astype(bf16)], axis=1)
        d_normed[rows, :] += jnp.dot(both, kvt_ref[0], preferred_element_type=f32)
        grad_kv = grad_kv + lax.dot_general(
            normed[rows, :], both, (((0,), (0,)), ((), ())), preferred_element_type=f32
        )
    attended = weighted_ref[0] * jnp.exp2(top_ref[0] - shift)
    for n in range(large_ref.shape[1]):
        lanes = slice(n * LANES, (n + 1) * LANES)
        large_ref[0, n, :LANES] = attended[:, lanes].astype(bf16)
        large_ref[0, n, LANES : 2 * LANES] = (grad_q[:, lanes] * scale).astype(bf16)
        large_ref[0, n, 2 * LANES :] = grad_kv[:, lanes].astype(bf16)

    @pl.when(pl.program_id(0) == pl.num_programs(0) - 1)
    def _():
        def body(a, carry):
            gg0, gg1 = carry
            c0, c1, inverse = norm_rows(mixed_ref[0, a], mixed_ref[1, a])
            rows = pl.ds(pl.multiple_of(a * tile_cols, tile_cols), tile_cols)
            d0 = d_normed[rows, :LANES]
            d1 = d_normed[rows, LANES:]
            gg0 = gg0 + jnp.sum(d0 * c0, axis=0, keepdims=True)
            gg1 = gg1 + jnp.sum(d1 * c1, axis=0, keepdims=True)
            s0 = d0 * gain_ref[:, :LANES]
            s1 = d1 * gain_ref[:, LANES:]
            mean = (
                jnp.sum(s0, axis=-1, keepdims=True) + jnp.sum(s1, axis=-1, keepdims=True)
            ) / (2 * LANES)
            dot = (
                jnp.sum(s0 * c0, axis=-1, keepdims=True) + jnp.sum(s1 * c1, axis=-1, keepdims=True)
            ) / (2 * LANES)
            m0 = inverse * (s0 - mean - c0 * dot)
            m1 = inverse * (s1 - mean - c1 * dot)
            d_mixed_ref[0, a] = m0.astype(bf16).astype(f32)
            d_mixed_ref[1, a] = m1.astype(bf16).astype(f32)
            return gg0, gg1

        zero = jnp.zeros((1, LANES), f32)
        gg0, gg1 = lax.fori_loop(0, tile_rows, body, (zero, zero))
        grad_gain_ref[:, :LANES] = gg0
        grad_gain_ref[:, LANES:] = gg1


def kernel_grad_kernel(tile_rows, tile_cols, x_ref, d_ref, out_ref, acc_ref):
    groups = tile_rows // GROUP
    acc_ref[...] = jnp.zeros_like(acc_ref)

    def body(n, carry):
        h = n // groups
        r0 = (n % groups) * GROUP
        for cb in range(tile_cols // 8):
            d = d_ref[h, pl.ds(r0, GROUP), cb * 8 : cb * 8 + 8, :]
            for j in range(KSIZE):
                x = x_ref[h, pl.ds(r0, GROUP + KSIZE - 1), cb * 8 + j : cb * 8 + j + 8, :].astype(f32)
                for i in range(KSIZE):
                    acc_ref[h, i * KSIZE + j] += jnp.sum(x[i : i + GROUP] * d, axis=0)
        return carry

    lax.fori_loop(0, 2 * groups, body, 0)
    out_ref[...] = jnp.sum(acc_ref[...], axis=2)


def transposed_kernel(tile_rows, tile_cols, d_ref, w_ref, patches_ref, patch_ref, bias_ref, out):
    conv_windows(d_ref, w_ref, out, tile_rows, tile_cols, True)
    for h in range(2):
        d = out[h].reshape(tile_rows * tile_cols, LANES).astype(bf16)
        patch_ref[:, h * LANES : (h + 1) * LANES] = jnp.dot(
            patches_ref[...], d, preferred_element_type=f32
        )
        bias_ref[:, h * LANES : (h + 1) * LANES] = jnp.sum(d.astype(f32), axis=0, keepdims=True)


MESH = pl.DeviceIdType.MESH


def greet(row, col, rows, cols):
    barrier = pltpu.get_barrier_semaphore()
    for p in range(1, cols):
        pl.semaphore_signal(
            barrier, inc=1, device_id=(row, lax.rem(col + p, cols)), device_id_type=MESH
        )
    for p in range(1, rows):
        pl.semaphore_signal(
            barrier, inc=1, device_id=(lax.rem(row + p, rows), col), device_id_type=MESH
        )
    pl.semaphore_wait(barrier, rows + cols - 2)


def push(src, dst, sems, stage, slot, device):
    copy = pltpu.make_async_remote_copy(
        src_ref=src,
        dst_ref=dst,
        send_sem=sems.at[0, stage, slot],
        recv_sem=sems.at[1, stage, slot],
        device_id=device,
        device_id_type=MESH,
    )
    copy.start()
    return copy


def await_into(dst, sems, stage, slot, device):
    pltpu.make_async_remote_copy(
        src_ref=dst,
        dst_ref=dst,
        send_sem=sems.at[0, stage, slot],
        recv_sem=sems.at[1, stage, slot],
        device_id=device,
        device_id_type=MESH,
    ).wait_recv()


def spread(out_ref, sems, row, col, rows, cols):
    copies = []
    for p in range(1, rows):
        there = (lax.rem(row + p, rows), col)
        copies.append(push(out_ref.at[col, row], out_ref.at[col, row], sems, 2, p, there))
    for p in range(1, rows):
        source = lax.rem(row + rows - p, rows)
        await_into(out_ref.at[col, source], sems, 2, p, (source, col))
    for p in range(1, cols):
        there = (row, lax.rem(col + p, cols))
        copies.append(push(out_ref.at[col], out_ref.at[col], sems, 3, p, there))
    for p in range(1, cols):
        source = lax.rem(col + cols - p, cols)
        await_into(out_ref.at[source], sems, 3, p, (row, source))
    for copy in copies:
        copy.wait_send()


def sum_kernel(x_ref, out_ref, first, middle, second, sems):
    cols, rows, n, _ = x_ref.shape
    row, col = lax.axis_index("rows"), lax.axis_index("cols")
    greet(row, col, rows, cols)
    copies = []
    for p in range(1, cols):
        there = lax.rem(col + p, cols)
        copies.append(push(x_ref.at[there], first.at[p], sems, 0, p, (row, there)))
    for p in range(1, cols):
        await_into(first.at[p], sems, 0, p, (row, lax.rem(col + cols - p, cols)))

    def body(r, carry):
        acc = x_ref[col, r].astype(f32)
        for p in range(1, cols):
            acc = acc + first[p, r].astype(f32)
        middle[r] = acc.astype(middle.dtype)
        return carry

    lax.fori_loop(0, rows, body, 0)
    for p in range(1, rows):
        there = lax.rem(row + p, rows)
        copies.append(push(middle.at[there], second.at[p], sems, 1, p, (there, col)))
    for p in range(1, rows):
        await_into(second.at[p], sems, 1, p, (lax.rem(row + rows - p, rows), col))
    acc = middle[row].astype(f32)
    for p in range(1, rows):
        acc = acc + second[p].astype(f32)
    out_ref[col, row] = acc.astype(out_ref.dtype)
    spread(out_ref, sems, row, col, rows, cols)
    for copy in copies:
        copy.wait_send()


def reduced(x, rows, cols, collective_id):
    count = x.shape[0]
    unit = rows * cols * (16 if x.dtype == bf16 else 8)
    padded = pl.cdiv(count, unit) * unit
    n = padded // (rows * cols)
    x = jnp.pad(x, ((0, padded - count), (0, 0))).reshape(cols, rows, n, LANES)
    vmem = pl.BlockSpec(memory_space=pltpu.VMEM)
    out = pl.pallas_call(
        sum_kernel,
        out_shape=jax.ShapeDtypeStruct(x.shape, x.dtype),
        in_specs=[vmem],
        out_specs=vmem,
        scratch_shapes=[
            pltpu.VMEM((cols, rows, n, LANES), x.dtype),
            pltpu.VMEM((rows, n, LANES), x.dtype),
            pltpu.VMEM((rows, n, LANES), x.dtype),
            pltpu.SemaphoreType.DMA((2, 4, max(rows, cols))),
        ],
        compiler_params=pltpu.CompilerParams(
            collective_id=collective_id, has_side_effects=True, vmem_limit_bytes=VMEM_LIMIT
        ),
        name="reduce" + str(collective_id),
    )(x)
    return out.reshape(padded, LANES)[:count]


def combine(stats):
    peak = jnp.max(stats[:, 0], axis=0)
    factor = jnp.exp2(stats[:, 0] - peak[None])
    return jnp.stack(
        [peak, jnp.sum(stats[:, 1] * factor, axis=0), jnp.sum(stats[:, 2] * factor, axis=0)]
    )


def stats_kernel(rows, cols, x_ref, out_ref, first, second, sems):
    row, col = lax.axis_index("rows"), lax.axis_index("cols")
    greet(row, col, rows, cols)
    copies = []
    first[0] = x_ref[...]
    for p in range(1, cols):
        there = (row, lax.rem(col + p, cols))
        copies.append(push(x_ref, first.at[p], sems, 0, p, there))
    for p in range(1, cols):
        await_into(first.at[p], sems, 0, p, (row, lax.rem(col + cols - p, cols)))
    second[0] = combine(first[...])
    for p in range(1, rows):
        there = (lax.rem(row + p, rows), col)
        copies.append(push(second.at[0], second.at[p], sems, 1, p, there))
    for p in range(1, rows):
        await_into(second.at[p], sems, 1, p, (lax.rem(row + rows - p, rows), col))
    total = combine(second[...])
    out_ref[0] = total[0] + jnp.log2(total[1])
    out_ref[1] = total[2] / total[1]
    for copy in copies:
        copy.wait_send()


def mesh_stats(x, rows, cols):
    vmem = pl.BlockSpec(memory_space=pltpu.VMEM)
    return pl.pallas_call(
        functools.partial(stats_kernel, rows, cols),
        out_shape=struct(2, *x.shape[1:]),
        in_specs=[vmem],
        out_specs=vmem,
        scratch_shapes=[
            pltpu.VMEM((cols,) + x.shape, f32),
            pltpu.VMEM((rows,) + x.shape, f32),
            pltpu.SemaphoreType.DMA((2, 2, max(rows, cols))),
        ],
        compiler_params=pltpu.CompilerParams(
            collective_id=1, has_side_effects=True, vmem_limit_bytes=VMEM_LIMIT
        ),
        name="stats",
    )(x)


def head_spec(shape):
    return pl.BlockSpec((1,) + shape, lambda n: (n, 0, 0))


def whole_spec(shape):
    return pl.BlockSpec(shape, lambda n: (0,) * len(shape))


def struct(*shape, dtype=f32):
    return jax.ShapeDtypeStruct(shape, dtype)


def per_device(
    pixels, patch_weight, patch_bias, conv_kernel, norm_gain, kv_weight, latents, d_attended
):
    tile_rows = pixels.shape[1] // PATCH
    tile_cols = pixels.shape[2] // PATCH
    tokens = tile_rows * tile_cols
    channels = patch_weight.shape[1]
    count, model_dim = latents.shape
    parts = count // LANES
    patches = patch_rows(pixels)
    embedded = (
        jnp.dot(patches, patch_weight, preferred_element_type=f32) + patch_bias
    ).astype(bf16)
    embedded = embedded.reshape(tile_rows, tile_cols, channels)
    sides = (("rows", 0), ("cols", 1))
    pad_rows, pad_cols = tile_rows + 2 * HALF, tile_cols + 8

    def windows(x):
        x = padded_2(x, sides, HALF)
        x = jnp.pad(x, ((0, 0), (0, 8 - 2 * HALF), (0, 0)))
        return halves(x).astype(f32)

    taps = KSIZE * KSIZE
    taps_w = conv_kernel.reshape(taps, 2, LANES).transpose(1, 0, 2)
    taps_w = jnp.broadcast_to(taps_w[:, :, None, :], (2, taps, 8, LANES))
    gain = norm_gain.reshape(1, channels)
    kv = kv_weight.reshape(channels, 2, HEADS, LANES).transpose(2, 0, 1, 3)
    kv = kv.reshape(HEADS, channels, 2 * LANES)
    kvt = kv.transpose(0, 2, 1)
    q = latents.reshape(count, HEADS, LANES).transpose(1, 0, 2)
    qt = q.transpose(0, 2, 1)
    da = d_attended.reshape(count, HEADS, LANES).transpose(1, 0, 2)
    dat = da.transpose(0, 2, 1)
    x = windows(embedded)
    params = pltpu.CompilerParams(vmem_limit_bytes=VMEM_LIMIT)
    mixed, proj, stats, weighted = pl.pallas_call(
        functools.partial(forward_kernel, tile_rows, tile_cols),
        grid=(HEADS,),
        in_specs=[
            whole_spec((2, pad_rows, pad_cols, LANES)),
            whole_spec((2, taps, 8, LANES)),
            whole_spec((1, channels)),
            head_spec((channels, 2 * LANES)),
            head_spec((LANES, count)),
            head_spec((LANES, count)),
        ],
        out_specs=[
            whole_spec((2, tile_rows, tile_cols, LANES)),
            head_spec((tokens, 2 * LANES)),
            pl.BlockSpec((3, 1, 1, count), lambda n: (0, n, 0, 0)),
            head_spec((LANES, count)),
        ],
        out_shape=[
            struct(2, tile_rows, tile_cols, LANES),
            struct(HEADS, tokens, 2 * LANES, dtype=bf16),
            struct(3, HEADS, 1, count),
            struct(HEADS, LANES, count),
        ],
        scratch_shapes=[pltpu.VMEM((tokens, channels), bf16), pltpu.VMEM((tokens, count), f32)],
        compiler_params=params,
        name="forward",
    )(x, taps_w, gain, kv, qt, dat)
    rows, cols = lax.axis_size("rows"), lax.axis_size("cols")
    shared = mesh_stats(stats.reshape(3, HEADS, count), rows, cols)
    shift, dots = shared.reshape(2, HEADS, 1, count)
    tops = stats[0]
    large, d_mixed, grad_gain = pl.pallas_call(
        functools.partial(backward_kernel, tile_rows, tile_cols),
        grid=(HEADS,),
        in_specs=[
            whole_spec((2, tile_rows, tile_cols, LANES)),
            whole_spec((1, channels)),
            head_spec((tokens, 2 * LANES)),
            head_spec((LANES, count)),
            head_spec((count, LANES)),
            head_spec((LANES, count)),
            head_spec((count, LANES)),
            head_spec((2 * LANES, channels)),
            head_spec((1, count)),
            head_spec((1, count)),
            head_spec((1, count)),
            head_spec((LANES, count)),
        ],
        out_specs=[
            pl.BlockSpec((1, parts, 4 * LANES, LANES), lambda n: (n, 0, 0, 0)),
            whole_spec((2, tile_rows, tile_cols, LANES)),
            whole_spec((1, channels)),
        ],
        out_shape=[
            struct(HEADS, parts, 4 * LANES, LANES, dtype=bf16),
            struct(2, tile_rows, tile_cols, LANES),
            struct(1, channels),
        ],
        scratch_shapes=[
            pltpu.VMEM((tokens, channels), bf16),
            pltpu.VMEM((8, LANES), bf16),
            pltpu.VMEM((tokens, channels), f32),
        ],
        compiler_params=params,
        name="backward",
    )(mixed, gain, proj, qt, q, dat, da, kvt, shift, dots, tops, weighted)
    large = reduced(large.reshape(-1, LANES), rows, cols, 2).astype(f32)
    large = large.reshape(HEADS, parts, 4 * LANES, LANES)
    d_tile = d_mixed.transpose(1, 2, 0, 3).reshape(tile_rows, tile_cols, channels).astype(bf16)
    d_padded = windows(d_tile)
    grad_kernel = pl.pallas_call(
        functools.partial(kernel_grad_kernel, tile_rows, tile_cols),
        out_shape=struct(2, taps, LANES),
        scratch_shapes=[pltpu.VMEM((2, taps, 8, LANES), f32)],
        compiler_params=params,
        name="kernel_grad",
    )(x, d_mixed)
    grad_patch, grad_bias = pl.pallas_call(
        functools.partial(transposed_kernel, tile_rows, tile_cols),
        out_shape=[struct(patches.shape[1], channels), struct(1, channels)],
        scratch_shapes=[pltpu.VMEM((2, tile_rows, tile_cols, LANES), f32)],
        compiler_params=params,
        name="transposed",
    )(d_padded, taps_w, patches.T)
    small = jnp.concatenate(
        [grad_kernel.transpose(1, 0, 2).reshape(taps, channels), grad_gain, grad_patch, grad_bias]
    )
    small = reduced(small.reshape(-1, LANES), rows, cols, 3).reshape(small.shape)
    attended = large[:, :, :LANES].transpose(1, 3, 0, 2).reshape(count, model_dim)
    grad_latents = large[:, :, LANES : 2 * LANES].transpose(1, 3, 0, 2).reshape(count, model_dim)
    grad_kv = large[:, :, 2 * LANES :].transpose(2, 1, 0, 3).reshape(channels, 2 * model_dim)
    return (
        attended,
        grad_latents,
        grad_kv,
        small[taps],
        small[:taps],
        small[taps + 1 : -1],
        small[-1],
    )


def solution(mesh):
    return jax.shard_map(
        per_device,
        mesh=mesh,
        in_specs=(P(None, "rows", "cols"), P(), P(), P(), P(), P(), P(), P()),
        out_specs=(P(), P(), P(), P(), P(), P(), P()),
        check_vma=False,
    )
```

time: 808 us -> 281 us (0.35)
  waiting for transfers between devices: 353 us -> 8 us
  Pallas kernels: 0 us -> 191 us
  matrix products: 122 us -> 0.47 us
  blocking collectives: 85.5 us -> 0 us
  local copies, waits for them, and re-layouts: 128 us -> 49.5 us
  other arithmetic: 79.9 us -> 10.2 us
  between operations: 15.6 us -> 1.05 us
    psum x3 -> x0, waiting for transfers between devices: 351 us -> none  [the longest x2 263 us: per_device(): lax.psum((local_latents, local_kv, local_gain, local_kernel, local_patch,...]
    pallas_call x0 -> x7, Pallas kernels: none -> 191 us  [the longest x2 79.6 us: reduced(): pl.pallas_call(sum_kernel, out_shape=jax.ShapeDtypeStruct(x.shape, x.dtyp...]
    dot_general x61 -> x1, matrix products: 122 us -> 0.47 us  [per_device(): jnp.dot(patches, patch_weight, preferred_element_type=f32) + patch_bias]
    reduce_sum x17 -> x0, other arithmetic: 71.2 us -> none  [the longest x1 21.4 us: per_device(): local_bias = jnp.sum(d_embedded.astype(jnp.float32), axis=0)]
    dynamic_update_slice x40 -> x0, local copies, waits for them, and re-layouts: 54.1 us -> none  [the longest x24 43.4 us: per_device(): lax.map(head_grads, (query_heads, key_heads, value_heads, top_score.T, su...]
    pmax x1 -> x0, blocking collectives: 44 us -> none  [per_device(): top_score = lax.pmax(local_top, ('rows', 'cols'))]
    psum x1 -> x0, blocking collectives: 41.5 us -> none  [per_device(): sum_exp, weighted = lax.psum((part_sum, part_weighted), ('rows', 'cols'))]
    reshape x3 -> x7, local copies, waits for them, and re-layouts: 14 us -> 4.17 us  [the longest x1 1.31 us: per_device(): kv = kv.reshape(HEADS, channels, 2 * LANES)]
  transfers between devices with their start and end apart: 11 -> 8, of which waited for: 5 -> 4; matrix products, arithmetic and copies ran while one was open for 4% -> 6% of each run, Pallas kernels for 0% -> 4%
where the time goes in v1:
time: 281 us; the launch traced here: 280 us
  Pallas kernels  191 us (68%)
  local copies, waits for them, and re-layouts  49.5 us (18%)
  starting transfers between devices  20 us (7%)
  other arithmetic  10.2 us (4%)
  waiting for transfers between devices  8 us (3%)
    pallas_call x2, Pallas kernels, reduced(): pl.pallas_call(sum_kernel, out_shape=jax.ShapeDtypeStruct(x.shape, x.dtyp...  79.6 us
    pallas_call x1, Pallas kernels, per_device(): pl.pallas_call(functools.partial(backward_kernel, tile_rows, tile_cols),...  38.8 us
    pallas_call x1, Pallas kernels, per_device(): pl.pallas_call(functools.partial(forward_kernel, tile_rows, tile_cols), g...  32.3 us
    pallas_call x1, Pallas kernels, mesh_stats(): pl.pallas_call(functools.partial(stats_kernel, rows, cols), out_shape=str...  17.7 us
    reshape x1, local copies, waits for them, and re-layouts, patch_rows(): pixels.reshape(in_channels, height // PATCH, PATCH, image_width // PATCH,...  15.2 us
    ppermute x4, starting transfers between devices, padded_2(): before = lax.ppermute(last, axis, up)  14.6 us
    pallas_call x1, Pallas kernels, per_device(): pl.pallas_call(functools.partial(transposed_kernel, tile_rows, tile_cols)...  12.2 us
    pallas_call x1, Pallas kernels, per_device(): pl.pallas_call(functools.partial(kernel_grad_kernel, tile_rows, tile_cols...  10.1 us
  transfers between devices with their start and end apart: 8, of which 4 were waited for; matrix products, arithmetic and copies ran while one was open for 6% of the time, Pallas kernels for 4%

profile of v1, /device:TPU:0, one launch (start us, length us, event | category | flops | bytes accessed | tf_op | source)
XLA Modules:
  0.0 279.9 jit_solution(16928247144127961732)
XLA Ops:
  0.6 15.2 %reshape.101 = bf16[3,32,4,64,4]{4,3,2,1,0:T(8,128)(2,1)} reshape(bf16[3,128,256]{2,1,0:T(8,128)(2,1)} %param.8) | data formatting | bytes 393216 | tf_op jit(solution)/shard_map/reshape | solution.py:39
  15.9 6.0 %copy.28 = bf16[32,64,3,4,4]{1,0,4,3,2:T(8,128)(2,1)S(1)} copy(bf16[32,64,3,4,4]{4,1,3,0,2:T(8,128)(2,1)} %bitcast.106) | data formatting | bytes 393216 | tf_op jit(solution)/shard_map/transpose | solution.py:40
  22.8 1.3 collective-permute-start.1
  24.1 5.6 %collective-permute-start = (bf16[3,64,256]{2,1,0:T(8,128)(2,1)S(1)}, bf16[3,64,256]{2,1,0:T(8,128)(2,1)S(1)}, u32[]{:S(2)}, u32[]{:S(2)}) collective-permute-start(bf16[3,64,256]{2,1,0:T(8,128)(2,1)S(1)} %bitcast.141), channel_id=1, source_target_pairs={{0,8},{8,16},{16,24},{1,9},{9,17},{17,25},{2,10},{10,18},{18,26},{... | collective-permute-start | bytes 294920 | tf_op jit(solution)/shard_map/ppermute | solution.py:31
  29.7 0.9 collective-permute-done.1
  30.6 1.3 collective-permute-done
  31.9 0.7 pad_maximum_fusion.3
  32.6 1.9 collective-permute-start.2
  34.5 1.3 collective-permute-start.3
  36.3 1.0 copy.36
  37.3 1.0 copy.35
  38.4 1.4 copy.55
  39.8 0.8 copy.31
  40.6 1.3 copy.34.kv_ref
  42.0 3.1 %bitcast_bitcast_fusion.1.x_ref = f32[2,38,72,128]{3,2,1,0:T(8,128)} fusion(bf16[38,3,256]{2,1,0:T(4,128)(2,1)} %collective-permute-done.3, bf16[38,3,256]{2,1,0:T(4,128)(2,1)} %collective-permute-done.2, bf16[3,64,256]{2,1,0:T(8,128)(2,1)S(1)} %collective-permute-done.1, bf16[32,64,256]{2,1,0:T(8,128)(2,1)S(1)} %bitcast.108, ...), kind=kLoop, calls=%fused_computation.1 | loop fusion | flops 11206656 | bytes 4163584 | tf_op jit(solution)/shard_map/convert_element_type | solution.py:435
  45.1 0.8 broadcast_in_dim.2.w_ref
  45.9 32.3 %forward.1 = (f32[2,32,64,128]{3,2,1,0:T(8,128)}, bf16[8,2048,256]{2,1,0:T(8,128)(2,1)}, f32[3,8,1,256]{3,2,1,0:T(1,128)}, f32[8,128,256]{2,1,0:T(8,128)}) custom-call(f32[2,38,72,128]{3,2,1,0:T(8,128)} %bitcast_bitcast_fusion.1.x_ref, f32[2,49,8,128]{3,2,1,0:T(8,128)} %broadcast_in_dim.2.w_ref, f32[1,256]{1,0:T(1,128)} %bitcast.143, ...), custom_call_target="tpu_custom_call" | custom-call | tf_op jit(solution)/shard_map/forward/pallas_call | solution.py:450
  78.2 1.3 slice_bitcast_fusion.5.top_ref
  79.5 1.3 copy.78
  80.8 17.7 %stats.1 = f32[2,8,256]{2,1,0:T(8,128)} custom-call(f32[3,8,256]{2,1,0:T(8,128)} %bitcast.140), custom_call_target="tpu_custom_call" | custom-call | tf_op jit(solution)/shard_map/stats/pallas_call | solution.py:386
  98.5 0.7 fusion.17
  99.8 38.8 %backward.1 = (bf16[8,2,512,128]{3,2,1,0:T(8,128)(2,1)}, f32[2,32,64,128]{3,2,1,0:T(8,128)}, f32[1,256]{1,0:T(1,128)}) custom-call(f32[2,32,64,128]{3,2,1,0:T(8,128)} %get-tuple-element.16.mixed_ref, f32[1,256]{1,0:T(1,128)} %bitcast.144, bf16[8,2048,256]{2,1,0:T(8,128)(2,1)} %get-tuple-element.17.proj_ref, bf16[8,128,256]{2,1,0:T(8,128)(2,1)} %bitcast.114, ...), custom_call_target="tpu_custom_call" | custom-call | tf_op jit(solution)/shard_map/backward/pallas_call | solution.py:481
  138.7 60.0 %reduce2.1 = bf16[8,4,256,128]{3,2,1,0:T(8,128)(2,1)} custom-call(bf16[8,4,256,128]{3,2,1,0:T(8,128)(2,1)} %bitcast.125), custom_call_target="tpu_custom_call" | custom-call | tf_op jit(solution)/shard_map/reduce2/pallas_call | solution.py:334
  198.7 2.1 bitcast_convert_fusion
  201.3 4.6 %collective-permute-start.4 = (bf16[3,64,256]{2,1,0:T(8,128)(2,1)S(1)}, bf16[3,64,256]{2,1,0:T(8,128)(2,1)S(1)}, u32[]{:S(2)}, u32[]{:S(2)}) collective-permute-start(bf16[3,64,256]{2,1,0:T(8,128)(2,1)S(1)} %bitcast.139), channel_id=1, source_target_pairs={{0,8},{8,16},{16,24},{1,9},{9,17},{17,25},{2,10},{10,18},{18,26},{... | collective-permute-start | bytes 294920 | tf_op jit(solution)/shard_map/ppermute | solution.py:31
  206.1 1.5 collective-permute-start.5
  207.6 1.3 collective-permute-done.4
  209.1 4.5 %collective-permute-done.5 = bf16[3,64,256]{2,1,0:T(8,128)(2,1)S(1)} collective-permute-done((bf16[3,64,256]{2,1,0:T(8,128)(2,1)S(1)}, bf16[3,64,256]{2,1,0:T(8,128)(2,1)S(1)}, u32[]{:S(2)}, u32[]{:S(2)}) %collective-permute-start.5) | collective-permute-done | bytes 98336 | tf_op jit(solution)/shard_map/ppermute | solution.py:32
  213.6 1.0 copy-done.6
  214.7 0.7 fusion.15
  215.3 2.5 collective-permute-start.6
  217.9 1.3 collective-permute-start.7
  219.2 1.5 slice_bitcast_fusion.1
  220.6 10.1 %kernel_grad.1 = f32[2,49,128]{2,1,0:T(8,128)} custom-call(f32[2,38,72,128]{3,2,1,0:T(8,128)} %bitcast_bitcast_fusion.1.x_ref, f32[2,32,64,128]{3,2,1,0:T(8,128)} %get-tuple-element.21.d_ref), custom_call_target="tpu_custom_call" | custom-call | tf_op jit(solution)/shard_map/kernel_grad/pallas_call | solution.py:520
  230.7 0.8 copy.42
  231.6 1.6 copy.40
  233.2 1.2 copy.73
  234.4 1.2 copy.41
  235.6 2.2 copy.72
  238.2 1.2 copy.74
  239.4 3.1 %bitcast_bitcast_fusion.d_ref = f32[2,38,72,128]{3,2,1,0:T(8,128)} fusion(bf16[38,3,256]{2,1,0:T(4,128)(2,1)} %collective-permute-done.7, bf16[38,64,256]{2,1,0:T(8,128)(2,1)S(1)} %copy-done.7, bf16[38,3,256]{2,1,0:T(4,128)(2,1)} %collective-permute-done.6), kind=kLoop, calls=%fused_computation | loop fusion | flops 7004160 | bytes 4163584 | tf_op jit(solution)/shard_map/convert_element_type | solution.py:435
  242.5 12.2 %transposed.1 = (f32[48,256]{1,0:T(8,128)}, f32[1,256]{1,0:T(1,128)}) custom-call(f32[2,38,72,128]{3,2,1,0:T(8,128)} %bitcast_bitcast_fusion.d_ref, f32[2,49,8,128]{3,2,1,0:T(8,128)} %broadcast_in_dim.2.w_ref, bf16[48,2048]{1,0:T(8,128)(2,1)} %bitcast.126), custom_call_target="tpu_custom_call" | custom-call | tf_op jit(solution)/shard_map/transposed/pallas_call | solution.py:527
  254.7 0.8 pad_maximum_fusion
  255.5 0.7 pad.13
  256.2 19.6 %reduce3.1 = f32[8,4,8,128]{3,2,1,0:T(8,128)} custom-call(f32[8,4,8,128]{3,2,1,0:T(8,128)} %bitcast.130), custom_call_target="tpu_custom_call" | custom-call | tf_op jit(solution)/shard_map/reduce3/pallas_call | solution.py:334
  275.8 1.3 slice_bitcast_fusion.6
  277.0 0.8 slice.108
  277.8 0.8 slice.107
  (53 shorter events, 4.4 us)
Async XLA Ops:
  0.6 21.7 %copy-start = (bf16[48,256]{1,0:T(8,128)(2,1)S(1)}, bf16[48,256]{1,0:T(8,128)(2,1)}, u32[]{:S(2)}) copy-start(bf16[48,256]{1,0:T(8,128)(2,1)} %param.9) | copy-start | bytes 73732
  15.9 6.4 %copy-start.13 = (f32[256]{0:T(256)S(1)}, f32[256]{0:T(256)}, u32[]{:S(2)}) copy-start(f32[256]{0:T(256)} %param.10) | copy-start | bytes 3076
  21.9 13.9 %copy-start.11 = (f32[49,256]{1,0:T(8,128)S(1)}, f32[49,256]{1,0:T(8,128)}, u32[]{:S(2)}) copy-start(f32[49,256]{1,0:T(8,128)} %param.11) | copy-start | bytes 150532
  21.9 13.9 %copy-start.9 = (bf16[256,1024]{1,0:T(8,128)(2,1)S(1)}, bf16[256,1024]{1,0:T(8,128)(2,1)}, u32[]{:S(2)}) copy-start(bf16[256,1024]{1,0:T(8,128)(2,1)} %param.14) | copy-start | bytes 1572868
  22.3 13.5 %copy-start.8 = (bf16[2048,48]{0,1:T(8,128)(2,1)}, bf16[2048,48]{0,1:T(8,128)(2,1)S(1)}, u32[]{:S(2)}) copy-start(bf16[2048,48]{0,1:T(8,128)(2,1)S(1)} %reshape.102) | copy-start | bytes 589828
  22.3 13.8 %copy-start.10 = (bf16[256,1024]{1,0:T(8,128)(2,1)S(1)}, bf16[256,1024]{1,0:T(8,128)(2,1)}, u32[]{:S(2)}) copy-start(bf16[256,1024]{1,0:T(8,128)(2,1)} %param.15) | copy-start | bytes 1572868
  22.8 7.7 %collective-permute-start.1 = (bf16[3,64,256]{2,1,0:T(8,128)(2,1)S(1)}, bf16[3,64,256]{2,1,0:T(8,128)(2,1)S(1)}, u32[]{:S(2)}, u32[]{:S(2)}) collective-permute-start(bf16[3,64,256]{2,1,0:T(8,128)(2,1)S(1)} %bitcast.142), channel_id=1, source_target_pairs={{8,0},{16,8},{24,16},{9,1},{17,9},{25,17},{10,2},{18,10},{26,18},{... | collective-permute-start | bytes 294920 | tf_op jit(solution)/shard_map/ppermute | solution.py:32
  24.1 7.8 %collective-permute-start = (bf16[3,64,256]{2,1,0:T(8,128)(2,1)S(1)}, bf16[3,64,256]{2,1,0:T(8,128)(2,1)S(1)}, u32[]{:S(2)}, u32[]{:S(2)}) collective-permute-start(bf16[3,64,256]{2,1,0:T(8,128)(2,1)S(1)} %bitcast.141), channel_id=1, source_target_pairs={{0,8},{8,16},{16,24},{1,9},{9,17},{17,25},{2,10},{10,18},{18,26},{... | collective-permute-start | bytes 294920 | tf_op jit(solution)/shard_map/ppermute | solution.py:31
  32.6 9.3 %collective-permute-start.2 = (bf16[38,3,256]{2,1,0:T(4,128)(2,1)}, bf16[38,3,256]{2,1,0:T(4,128)(2,1)}, u32[]{:S(2)}, u32[]{:S(2)}) collective-permute-start(bf16[38,3,256]{2,1,0:T(4,128)(2,1)} %get-tuple-element.31), channel_id=1, source_target_pairs={{0,1},{1,2},{2,3},{3,4},{4,5},{5,6},{6,7},{8,9},{9,10},{10,11},{11... | collective-permute-start | bytes 175112 | tf_op jit(solution)/shard_map/ppermute | solution.py:31
  34.5 7.4 %collective-permute-start.3 = (bf16[38,3,256]{2,1,0:T(4,128)(2,1)S(1)}, bf16[38,3,256]{2,1,0:T(4,128)(2,1)}, u32[]{:S(2)}, u32[]{:S(2)}) collective-permute-start(bf16[38,3,256]{2,1,0:T(4,128)(2,1)S(1)} %get-tuple-element.32), channel_id=1, source_target_pairs={{1,0},{2,1},{3,2},{4,3},{5,4},{6,5},{7,6},{9,8},{10,9},{11,10},{12... | collective-permute-start | bytes 175112 | tf_op jit(solution)/shard_map/ppermute | solution.py:32
  36.1 3.7 %copy-start.2 = (bf16[256,1024]{0,1:T(8,128)(2,1)}, bf16[256,1024]{0,1:T(8,128)(2,1)S(1)}, u32[]{:S(2)}) copy-start(bf16[256,1024]{0,1:T(8,128)(2,1)S(1)} %copy.32) | copy-start | bytes 1572868
  36.3 3.5 %copy-start.3 = (bf16[256,1024]{0,1:T(8,128)(2,1)}, bf16[256,1024]{0,1:T(8,128)(2,1)S(1)}, u32[]{:S(2)}) copy-start(bf16[256,1024]{0,1:T(8,128)(2,1)S(1)} %copy.33) | copy-start | bytes 1572868
  40.6 4.5 %copy-start.1 = (bf16[256,2,8,128]{0,3,1,2:T(8,128)(2,1)}, bf16[256,2,8,128]{0,3,1,2:T(8,128)(2,1)S(1)}, u32[]{:S(2)}) copy-start(bf16[256,2,8,128]{0,3,1,2:T(8,128)(2,1)S(1)} %copy.31) | copy-start | bytes 3145732
  198.7 2.2 copy-start.4
  201.3 7.6 %collective-permute-start.4 = (bf16[3,64,256]{2,1,0:T(8,128)(2,1)S(1)}, bf16[3,64,256]{2,1,0:T(8,128)(2,1)S(1)}, u32[]{:S(2)}, u32[]{:S(2)}) collective-permute-start(bf16[3,64,256]{2,1,0:T(8,128)(2,1)S(1)} %bitcast.139), channel_id=1, source_target_pairs={{0,8},{8,16},{16,24},{1,9},{9,17},{17,25},{2,10},{10,18},{18,26},{... | collective-permute-start | bytes 294920 | tf_op jit(solution)/shard_map/ppermute | solution.py:31
  206.1 7.5 %collective-permute-start.5 = (bf16[3,64,256]{2,1,0:T(8,128)(2,1)S(1)}, bf16[3,64,256]{2,1,0:T(8,128)(2,1)S(1)}, u32[]{:S(2)}, u32[]{:S(2)}) collective-permute-start(bf16[3,64,256]{2,1,0:T(8,128)(2,1)S(1)} %bitcast.138), channel_id=1, source_target_pairs={{8,0},{16,8},{24,16},{9,1},{17,9},{25,17},{10,2},{18,10},{26,18},{... | collective-permute-start | bytes 294920 | tf_op jit(solution)/shard_map/ppermute | solution.py:32
  213.6 1.1 copy-start.6
  215.3 24.1 %collective-permute-start.6 = (bf16[38,3,256]{2,1,0:T(4,128)(2,1)}, bf16[38,3,256]{2,1,0:T(4,128)(2,1)}, u32[]{:S(2)}, u32[]{:S(2)}) collective-permute-start(bf16[38,3,256]{2,1,0:T(4,128)(2,1)} %get-tuple-element.29), channel_id=1, source_target_pairs={{0,1},{1,2},{2,3},{3,4},{4,5},{5,6},{6,7},{8,9},{9,10},{10,11},{11... | collective-permute-start | bytes 175112 | tf_op jit(solution)/shard_map/ppermute | solution.py:31
  217.9 21.6 %collective-permute-start.7 = (bf16[38,3,256]{2,1,0:T(4,128)(2,1)S(1)}, bf16[38,3,256]{2,1,0:T(4,128)(2,1)}, u32[]{:S(2)}, u32[]{:S(2)}) collective-permute-start(bf16[38,3,256]{2,1,0:T(4,128)(2,1)S(1)} %get-tuple-element.30), channel_id=1, source_target_pairs={{1,0},{2,1},{3,2},{4,3},{5,4},{6,5},{7,6},{9,8},{10,9},{11,10},{12... | collective-permute-start | bytes 175112 | tf_op jit(solution)/shard_map/ppermute | solution.py:32
  235.6 2.2 copy-start.5
  237.8 1.6 copy-start.7
  242.5 12.2 %copy-start.12 = (f32[1,256]{1,0:T(1,128)S(1)}, f32[1,256]{1,0:T(1,128)}, u32[]{:S(2)}) copy-start(f32[1,256]{1,0:T(1,128)} %get-tuple-element.22) | copy-start | bytes 3076

commit v2 on v1

--- a/solution.py
+++ b/solution.py
@@ -11,6 +11,7 @@
 KSIZE = 7
 HEADS = 8
 HALF = KSIZE // 2
+EDGE = 8 - HALF
 LANES = 128
 GROUP = 8
 LOG2E = 1.4426950408889634
@@ -21,41 +22,28 @@
 bf16 = jnp.bfloat16
 
 
-def padded_2(x, sides, width):
-    for axis, dim in sides:
-        devices, length = (lax.axis_size(axis), x.shape[dim])
-        up = [(i, (i + 1) % devices) for i in range(devices - 1)]
-        down = [(j, i) for i, j in up]
-        last = lax.slice_in_dim(x, length - width, length, axis=dim)
-        leading = lax.slice_in_dim(x, 0, width, axis=dim)
-        before = lax.ppermute(last, axis, up)
-        after = lax.ppermute(leading, axis, down)
-        x = jnp.concatenate([before, x, after], axis=dim)
-    return x
-
-
-def patch_rows(pixels):
-    in_channels, height, image_width = pixels.shape
-    blocks = pixels.reshape(in_channels, height // PATCH, PATCH, image_width // PATCH, PATCH)
-    blocks = blocks.transpose(1, 3, 0, 2, 4)
-    return blocks.reshape(height // PATCH * (image_width // PATCH), in_channels * PATCH * PATCH)
-
-
-def halves(x):
-    rows, cols, channels = x.shape
-    return x.reshape(rows, cols, channels // LANES, LANES).transpose(2, 0, 1, 3)
-
-
-def conv_windows(x_ref, w_ref, out_ref, tile_rows, tile_cols, flipped):
+def patch_columns(pixels):
+    fields, height, width = pixels.shape
+    place = jnp.arange(width)
+    target = (place % PATCH) * (width // PATCH) + place // PATCH
+    sort = (target[:, None] == place[None, :]).astype(bf16)
+    x = jnp.dot(pixels.reshape(fields * height, width), sort, preferred_element_type=f32)
+    x = x.astype(bf16).reshape(fields, height // PATCH, PATCH, PATCH, width // PATCH)
+    x = x.transpose(0, 2, 3, 1, 4)
+    return x.reshape(fields * PATCH * PATCH, height // PATCH * (width // PATCH))
+
+
+def conv_windows(x_ref, w_ref, out_ref, tile_rows, tile_cols, flipped, part=None):
     groups = tile_rows // GROUP
+    first, last = (0, 2 * groups) if part is None else (part * groups, (part + 1) * groups)
 
     def body(n, carry):
         h = n // groups
         r0 = (n % groups) * GROUP
         for cb in range(tile_cols // 8):
-            acc = x_ref[h, pl.ds(r0 + HALF, GROUP), cb * 8 + HALF : cb * 8 + HALF + 8, :].astype(f32)
+            acc = x_ref[h, pl.ds(r0 + HALF, GROUP), cb * 8 + 8 : cb * 8 + 16, :].astype(f32)
             for j in range(KSIZE):
-                x = x_ref[h, pl.ds(r0, GROUP + KSIZE - 1), cb * 8 + j : cb * 8 + j + 8, :].astype(f32)
+                x = x_ref[h, pl.ds(r0, GROUP + KSIZE - 1), cb * 8 + EDGE + j : cb * 8 + EDGE + j + 8, :].astype(f32)
                 for i in range(KSIZE):
                     tap = i * KSIZE + j
                     if flipped:
@@ -64,7 +52,7 @@
             out_ref[h, pl.ds(r0, GROUP), cb * 8 : cb * 8 + 8, :] = acc
         return carry
 
-    lax.fori_loop(0, 2 * groups, body, 0)
+    lax.fori_loop(first, last, body, 0)
 
 
 def norm_rows(m0, m1):
@@ -204,33 +192,21 @@
         grad_gain_ref[:, LANES:] = gg1
 
 
-def kernel_grad_kernel(tile_rows, tile_cols, x_ref, d_ref, out_ref, acc_ref):
-    groups = tile_rows // GROUP
-    acc_ref[...] = jnp.zeros_like(acc_ref)
+def kernel_grad(x_ref, d_ref, acc_ref, tile_rows, tile_cols, h):
+    acc_ref[h] = jnp.zeros(acc_ref.shape[1:], f32)
 
     def body(n, carry):
-        h = n // groups
-        r0 = (n % groups) * GROUP
+        r0 = n * GROUP
         for cb in range(tile_cols // 8):
-            d = d_ref[h, pl.ds(r0, GROUP), cb * 8 : cb * 8 + 8, :]
+            d = d_ref[h, pl.ds(r0 + HALF, GROUP), cb * 8 + 8 : cb * 8 + 16, :]
             for j in range(KSIZE):
-                x = x_ref[h, pl.ds(r0, GROUP + KSIZE - 1), cb * 8 + j : cb * 8 + j + 8, :].astype(f32)
+                lanes = slice(cb * 8 + EDGE + j, cb * 8 + EDGE + j + 8)
+                x = x_ref[h, pl.ds(r0, GROUP + KSIZE - 1), lanes, :]
                 for i in range(KSIZE):
                     acc_ref[h, i * KSIZE + j] += jnp.sum(x[i : i + GROUP] * d, axis=0)
         return carry
 
-    lax.fori_loop(0, 2 * groups, body, 0)
-    out_ref[...] = jnp.sum(acc_ref[...], axis=2)
-
-
-def transposed_kernel(tile_rows, tile_cols, d_ref, w_ref, patches_ref, patch_ref, bias_ref, out):
-    conv_windows(d_ref, w_ref, out, tile_rows, tile_cols, True)
-    for h in range(2):
-        d = out[h].reshape(tile_rows * tile_cols, LANES).astype(bf16)
-        patch_ref[:, h * LANES : (h + 1) * LANES] = jnp.dot(
-            patches_ref[...], d, preferred_element_type=f32
-        )
-        bias_ref[:, h * LANES : (h + 1) * LANES] = jnp.sum(d.astype(f32), axis=0, keepdims=True)
+    lax.fori_loop(0, tile_rows // GROUP, body, 0)
 
 
 MESH = pl.DeviceIdType.MESH
@@ -273,81 +249,234 @@
     ).wait_recv()
 
 
-def spread(out_ref, sems, row, col, rows, cols):
-    copies = []
-    for p in range(1, rows):
-        there = (lax.rem(row + p, rows), col)
-        copies.append(push(out_ref.at[col, row], out_ref.at[col, row], sems, 2, p, there))
-    for p in range(1, rows):
-        source = lax.rem(row + rows - p, rows)
-        await_into(out_ref.at[col, source], sems, 2, p, (source, col))
-    for p in range(1, cols):
-        there = (row, lax.rem(col + p, cols))
-        copies.append(push(out_ref.at[col], out_ref.at[col], sems, 3, p, there))
-    for p in range(1, cols):
-        source = lax.rem(col + cols - p, cols)
-        await_into(out_ref.at[source], sems, 3, p, (row, source))
-    for copy in copies:
-        copy.wait_send()
-
-
-def sum_kernel(x_ref, out_ref, first, middle, second, sems):
-    cols, rows, n, _ = x_ref.shape
+def halo_cols(buf, sems, row, col, cols, tile_rows, tile_cols):
+    inner = pl.ds(HALF, tile_rows)
+
+    def part(start):
+        return buf.at[:, inner, pl.ds(start, 8), :]
+
+    def copies():
+        right = pltpu.make_async_remote_copy(
+            src_ref=part(tile_cols), dst_ref=part(0), send_sem=sems.at[0, 0], recv_sem=sems.at[1, 0],
+            device_id=(row, lax.min(col + 1, cols - 1)), device_id_type=MESH,
+        )
+        left = pltpu.make_async_remote_copy(
+            src_ref=part(8), dst_ref=part(tile_cols + 8), send_sem=sems.at[0, 1], recv_sem=sems.at[1, 1],
+            device_id=(row, lax.max(col - 1, 0)), device_id_type=MESH,
+        )
+        return right, left
+
+    return run_halo(copies, col, cols)
+
+
+def halo_rows(buf, sems, row, col, rows, tile_rows):
+    def part(start):
+        return buf.at[:, pl.ds(start, HALF), :, :]
+
+    def copies():
+        down = pltpu.make_async_remote_copy(
+            src_ref=part(tile_rows), dst_ref=part(0), send_sem=sems.at[0, 2], recv_sem=sems.at[1, 2],
+            device_id=(lax.min(row + 1, rows - 1), col), device_id_type=MESH,
+        )
+        up = pltpu.make_async_remote_copy(
+            src_ref=part(HALF), dst_ref=part(tile_rows + HALF), send_sem=sems.at[0, 3], recv_sem=sems.at[1, 3],
+            device_id=(lax.max(row - 1, 0), col), device_id_type=MESH,
+        )
+        return down, up
+
+    return run_halo(copies, row, rows)
+
+
+def run_halo(copies, me, devices):
+    @pl.when(me < devices - 1)
+    def _():
+        copies()[0].start()
+
+    @pl.when(me > 0)
+    def _():
+        copies()[1].start()
+
+    def wait():
+        @pl.when(me > 0)
+        def _():
+            copies()[0].wait_recv()
+            copies()[1].wait_send()
+
+        @pl.when(me < devices - 1)
+        def _():
+            copies()[1].wait_recv()
+            copies()[0].wait_send()
+
+    return wait
+
+
+class Reduction:
+    def __init__(self, x, out, first, middle, second, sems):
+        self.x, self.out, self.first, self.middle, self.second = x, out, first, middle, second
+        self.sems = sems
+        self.cols, self.rows = x.shape[:2]
+        self.row, self.col = lax.axis_index("rows"), lax.axis_index("cols")
+        self.copies = []
+
+    def across(self, p):
+        return lax.rem(self.col + p, self.cols)
+
+    def along(self, p):
+        return lax.rem(self.row + p, self.rows)
+
+    def send_0(self):
+        for p in range(1, self.cols):
+            there = self.across(p)
+            self.copies.append(
+                push(self.x.at[there], self.first.at[p], self.sems, 0, p, (self.row, there))
+            )
+
+    def sum_0(self):
+        for p in range(1, self.cols):
+            source = (self.row, self.across(self.cols - p))
+            await_into(self.first.at[p], self.sems, 0, p, source)
+
+        def body(r, carry):
+            acc = self.x[self.col, r].astype(f32)
+            for p in range(1, self.cols):
+                acc = acc + self.first[p, r].astype(f32)
+            self.middle[r] = acc.astype(self.middle.dtype)
+            return carry
+
+        lax.fori_loop(0, self.rows, body, 0)
+        for p in range(1, self.rows):
+            there = self.along(p)
+            self.copies.append(
+                push(self.middle.at[there], self.second.at[p], self.sems, 1, p, (there, self.col))
+            )
+
+    def sum_1(self):
+        for p in range(1, self.rows):
+            source = (self.along(self.rows - p), self.col)
+            await_into(self.second.at[p], self.sems, 1, p, source)
+        acc = self.middle[self.row].astype(f32)
+        for p in range(1, self.rows):
+            acc = acc + self.second[p].astype(f32)
+        self.out[self.col, self.row] = acc.astype(self.out.dtype)
+        piece = self.out.at[self.col, self.row]
+        for p in range(1, self.rows):
+            self.copies.append(push(piece, piece, self.sems, 2, p, (self.along(p), self.col)))
+
+    def spread_2(self):
+        for p in range(1, self.rows):
+            source = self.along(self.rows - p)
+            await_into(self.out.at[self.col, source], self.sems, 2, p, (source, self.col))
+        slab = self.out.at[self.col]
+        for p in range(1, self.cols):
+            self.copies.append(push(slab, slab, self.sems, 3, p, (self.row, self.across(p))))
+
+    def spread_3(self):
+        for p in range(1, self.cols):
+            source = self.across(self.cols - p)
+            await_into(self.out.at[source], self.sems, 3, p, (self.row, source))
+        for copy in self.copies:
+            copy.wait_send()
+
+
+def embed_kernel(rows, cols, tile_rows, tile_cols, patches_ref, w_ref, bias_ref, out_ref, buf, sems):
     row, col = lax.axis_index("rows"), lax.axis_index("cols")
+    embedded = lax.dot_general(
+        patches_ref[...], w_ref[...], (((0,), (0,)), ((), ())), preferred_element_type=f32
+    )
+    embedded = (embedded + bias_ref[...]).astype(bf16).astype(f32)
+    buf[...] = jnp.zeros_like(buf)
+    for h in range(2):
+        tile = embedded[:, h * LANES : (h + 1) * LANES].reshape(tile_rows, tile_cols, LANES)
+        buf[h, HALF : HALF + tile_rows, 8 : 8 + tile_cols, :] = tile
     greet(row, col, rows, cols)
-    copies = []
-    for p in range(1, cols):
-        there = lax.rem(col + p, cols)
-        copies.append(push(x_ref.at[there], first.at[p], sems, 0, p, (row, there)))
-    for p in range(1, cols):
-        await_into(first.at[p], sems, 0, p, (row, lax.rem(col + cols - p, cols)))
-
-    def body(r, carry):
-        acc = x_ref[col, r].astype(f32)
-        for p in range(1, cols):
-            acc = acc + first[p, r].astype(f32)
-        middle[r] = acc.astype(middle.dtype)
-        return carry
-
-    lax.fori_loop(0, rows, body, 0)
-    for p in range(1, rows):
-        there = lax.rem(row + p, rows)
-        copies.append(push(middle.at[there], second.at[p], sems, 1, p, (there, col)))
-    for p in range(1, rows):
-        await_into(second.at[p], sems, 1, p, (lax.rem(row + rows - p, rows), col))
-    acc = middle[row].astype(f32)
-    for p in range(1, rows):
-        acc = acc + second[p].astype(f32)
-    out_ref[col, row] = acc.astype(out_ref.dtype)
-    spread(out_ref, sems, row, col, rows, cols)
-    for copy in copies:
-        copy.wait_send()
-
-
-def reduced(x, rows, cols, collective_id):
-    count = x.shape[0]
-    unit = rows * cols * (16 if x.dtype == bf16 else 8)
-    padded = pl.cdiv(count, unit) * unit
-    n = padded // (rows * cols)
-    x = jnp.pad(x, ((0, padded - count), (0, 0))).reshape(cols, rows, n, LANES)
+    halo_cols(buf, sems, row, col, cols, tile_rows, tile_cols)()
+    halo_rows(buf, sems, row, col, rows, tile_rows)()
+    out_ref[...] = buf[...]
+
+
+def closing_kernel(
+    tile_rows, tile_cols, large_ref, x_ref, d_ref, w_ref, patches_ref, gain_ref,
+    large_out, small_out,
+    buf, acc, out, flat, small, first, middle, second, s_first, s_middle, s_second,
+    halo_sems, sems, s_sems,
+):
+    cols, rows = large_ref.shape[:2]
+    row, col = lax.axis_index("rows"), lax.axis_index("cols")
+    taps = KSIZE * KSIZE
+    buf[...] = jnp.zeros_like(buf)
+    buf[:, HALF : HALF + tile_rows, 8 : 8 + tile_cols, :] = d_ref[...]
+    flat[...] = jnp.zeros_like(flat)
+    greet(row, col, rows, cols)
+    big = Reduction(large_ref, large_out, first, middle, second, sems)
+    little = Reduction(small, small_out, s_first, s_middle, s_second, s_sems)
+    wait = halo_cols(buf, halo_sems, row, col, cols, tile_rows, tile_cols)
+    big.send_0()
+    kernel_grad(x_ref, d_ref=buf, acc_ref=acc, tile_rows=tile_rows, tile_cols=tile_cols, h=0)
+    wait()
+    wait = halo_rows(buf, halo_sems, row, col, rows, tile_rows)
+    kernel_grad(x_ref, d_ref=buf, acc_ref=acc, tile_rows=tile_rows, tile_cols=tile_cols, h=1)
+    wait()
+    patch_size = patches_ref.shape[0]
+    part = flat.shape[0] // 2
+    for h in range(2):
+        conv_windows(buf, w_ref, out, tile_rows, tile_cols, True, h)
+        d = out[h].reshape(tile_rows * tile_cols, LANES).astype(bf16)
+        base = h * part
+        flat[base : base + patch_size, :] = jnp.dot(
+            patches_ref[...], d, preferred_element_type=f32
+        )
+        flat[base + patch_size : base + patch_size + taps, :] = jnp.sum(acc[h], axis=1)
+        flat[base + part - 2 : base + part - 1, :] = jnp.sum(d.astype(f32), axis=0, keepdims=True)
+        flat[base + part - 1 : base + part, :] = gain_ref[:, h * LANES : (h + 1) * LANES]
+        if h == 0:
+            big.sum_0()
+    for n in range(cols * rows):
+        block = small.shape[2]
+        small[n // rows, n % rows] = flat[n * block : (n + 1) * block, :]
+    little.send_0()
+    big.sum_1()
+    little.sum_0()
+    big.spread_2()
+    little.sum_1()
+    little.spread_2()
+    little.spread_3()
+    big.spread_3()
+
+
+def closing(large, x, d_mixed, taps_w, patches_t, grad_gain, rows, cols):
+    _, tile_rows, tile_cols, _ = d_mixed.shape
+    n = large.size // (rows * cols * LANES)
+    large = large.reshape(cols, rows, n, LANES)
+    pieces = rows * cols
+    needed = 2 * (patches_t.shape[0] + KSIZE * KSIZE + 2)
+    m = pl.cdiv(needed, pieces * 8) * 8
     vmem = pl.BlockSpec(memory_space=pltpu.VMEM)
-    out = pl.pallas_call(
-        sum_kernel,
-        out_shape=jax.ShapeDtypeStruct(x.shape, x.dtype),
-        in_specs=[vmem],
-        out_specs=vmem,
+    return pl.pallas_call(
+        functools.partial(closing_kernel, tile_rows, tile_cols),
+        out_shape=[struct(cols, rows, n, LANES, dtype=bf16), struct(cols, rows, m, LANES)],
+        in_specs=[vmem] * 6,
+        out_specs=[vmem] * 2,
         scratch_shapes=[
-            pltpu.VMEM((cols, rows, n, LANES), x.dtype),
-            pltpu.VMEM((rows, n, LANES), x.dtype),
-            pltpu.VMEM((rows, n, LANES), x.dtype),
+            pltpu.VMEM((2, tile_rows + 2 * HALF, tile_cols + 16, LANES), f32),
+            pltpu.VMEM((2, KSIZE * KSIZE, 8, LANES), f32),
+            pltpu.VMEM((2, tile_rows, tile_cols, LANES), f32),
+            pltpu.VMEM((pieces * m, LANES), f32),
+            pltpu.VMEM((cols, rows, m, LANES), f32),
+            pltpu.VMEM((cols, rows, n, LANES), bf16),
+            pltpu.VMEM((rows, n, LANES), bf16),
+            pltpu.VMEM((rows, n, LANES), bf16),
+            pltpu.VMEM((cols, rows, m, LANES), f32),
+            pltpu.VMEM((rows, m, LANES), f32),
+            pltpu.VMEM((rows, m, LANES), f32),
+            pltpu.SemaphoreType.DMA((2, 4)),
             pltpu.SemaphoreType.DMA((2, 4, max(rows, cols))),
+            pltpu.SemaphoreType.DMA((2, 4, max(rows, cols))),
         ],
         compiler_params=pltpu.CompilerParams(
-            collective_id=collective_id, has_side_effects=True, vmem_limit_bytes=VMEM_LIMIT
+            collective_id=2, has_side_effects=True, vmem_limit_bytes=VMEM_LIMIT
         ),
-        name="reduce" + str(collective_id),
-    )(x)
-    return out.reshape(padded, LANES)[:count]
+        name="closing",
+    )(large, x, d_mixed, taps_w, patches_t, grad_gain)
 
 
 def combine(stats):
@@ -421,18 +550,24 @@
     channels = patch_weight.shape[1]
     count, model_dim = latents.shape
     parts = count // LANES
-    patches = patch_rows(pixels)
-    embedded = (
-        jnp.dot(patches, patch_weight, preferred_element_type=f32) + patch_bias
-    ).astype(bf16)
-    embedded = embedded.reshape(tile_rows, tile_cols, channels)
-    sides = (("rows", 0), ("cols", 1))
-    pad_rows, pad_cols = tile_rows + 2 * HALF, tile_cols + 8
-
-    def windows(x):
-        x = padded_2(x, sides, HALF)
-        x = jnp.pad(x, ((0, 0), (0, 8 - 2 * HALF), (0, 0)))
-        return halves(x).astype(f32)
+    rows, cols = lax.axis_size("rows"), lax.axis_size("cols")
+    patches_t = patch_columns(pixels)
+    pad_rows, pad_cols = tile_rows + 2 * HALF, tile_cols + 16
+    vmem = pl.BlockSpec(memory_space=pltpu.VMEM)
+    x = pl.pallas_call(
+        functools.partial(embed_kernel, rows, cols, tile_rows, tile_cols),
+        out_shape=struct(2, pad_rows, pad_cols, LANES),
+        in_specs=[vmem] * 3,
+        out_specs=vmem,
+        scratch_shapes=[
+            pltpu.VMEM((2, pad_rows, pad_cols, LANES), f32),
+            pltpu.SemaphoreType.DMA((2, 4)),
+        ],
+        compiler_params=pltpu.CompilerParams(
+            collective_id=3, has_side_effects=True, vmem_limit_bytes=VMEM_LIMIT
+        ),
+        name="embed",
+    )(patches_t, patch_weight, patch_bias.reshape(1, channels))
 
     taps = KSIZE * KSIZE
     taps_w = conv_kernel.reshape(taps, 2, LANES).transpose(1, 0, 2)
@@ -445,7 +580,6 @@
     qt = q.transpose(0, 2, 1)
     da = d_attended.reshape(count, HEADS, LANES).transpose(1, 0, 2)
     dat = da.transpose(0, 2, 1)
-    x = windows(embedded)
     params = pltpu.CompilerParams(vmem_limit_bytes=VMEM_LIMIT)
     mixed, proj, stats, weighted = pl.pallas_call(
         functools.partial(forward_kernel, tile_rows, tile_cols),
@@ -474,7 +608,6 @@
         compiler_params=params,
         name="forward",
     )(x, taps_w, gain, kv, qt, dat)
-    rows, cols = lax.axis_size("rows"), lax.axis_size("cols")
     shared = mesh_stats(stats.reshape(3, HEADS, count), rows, cols)
     shift, dots = shared.reshape(2, HEADS, 1, count)
     tops = stats[0]
@@ -513,28 +646,11 @@
         compiler_params=params,
         name="backward",
     )(mixed, gain, proj, qt, q, dat, da, kvt, shift, dots, tops, weighted)
-    large = reduced(large.reshape(-1, LANES), rows, cols, 2).astype(f32)
-    large = large.reshape(HEADS, parts, 4 * LANES, LANES)
-    d_tile = d_mixed.transpose(1, 2, 0, 3).reshape(tile_rows, tile_cols, channels).astype(bf16)
-    d_padded = windows(d_tile)
-    grad_kernel = pl.pallas_call(
-        functools.partial(kernel_grad_kernel, tile_rows, tile_cols),
-        out_shape=struct(2, taps, LANES),
-        scratch_shapes=[pltpu.VMEM((2, taps, 8, LANES), f32)],
-        compiler_params=params,
-        name="kernel_grad",
-    )(x, d_mixed)
-    grad_patch, grad_bias = pl.pallas_call(
-        functools.partial(transposed_kernel, tile_rows, tile_cols),
-        out_shape=[struct(patches.shape[1], channels), struct(1, channels)],
-        scratch_shapes=[pltpu.VMEM((2, tile_rows, tile_cols, LANES), f32)],
-        compiler_params=params,
-        name="transposed",
-    )(d_padded, taps_w, patches.T)
-    small = jnp.concatenate(
-        [grad_kernel.transpose(1, 0, 2).reshape(taps, channels), grad_gain, grad_patch, grad_bias]
-    )
-    small = reduced(small.reshape(-1, LANES), rows, cols, 3).reshape(small.shape)
+    large, small = closing(large, x, d_mixed, taps_w, patches_t, grad_gain, rows, cols)
+    large = large.astype(f32).reshape(HEADS, parts, 4 * LANES, LANES)
+    half_rows = small.size // (2 * LANES)
+    small = small.reshape(2, half_rows, LANES).transpose(1, 0, 2).reshape(half_rows, channels)
+    size = patches_t.shape[0]
     attended = large[:, :, :LANES].transpose(1, 3, 0, 2).reshape(count, model_dim)
     grad_latents = large[:, :, LANES : 2 * LANES].transpose(1, 3, 0, 2).reshape(count, model_dim)
     grad_kv = large[:, :, 2 * LANES :].transpose(2, 1, 0, 3).reshape(channels, 2 * model_dim)
@@ -542,10 +658,10 @@
         attended,
         grad_latents,
         grad_kv,
-        small[taps],
-        small[:taps],
-        small[taps + 1 : -1],
         small[-1],
+        small[size : size + taps],
+        small[:size],
+        small[-2],
     )
 
 

time: 281 us -> 205 us (0.73)
  local copies, waits for them, and re-layouts: 49.5 us -> 26.5 us
  starting transfers between devices: 20 us -> 0 us
  Pallas kernels: 191 us -> 175 us
  other arithmetic: 10.2 us -> 2.01 us
  waiting for transfers between devices: 8 us -> 0 us
    ppermute x8 -> x0, starting transfers between devices: 20 us -> none  [the longest x4 14.6 us: padded_2(): before = lax.ppermute(last, axis, up)]
    pallas_call x4 -> x2, Pallas kernels: 102 us -> 86.4 us  [the longest x1 72 us: closing(): pl.pallas_call(functools.partial(closing_kernel, tile_rows, tile_cols), o...]
    reshape x3 -> x2, local copies, waits for them, and re-layouts: 15.6 us -> 1.28 us  [the longest x1 1.07 us: patch_columns(): return x.reshape(fields * PATCH * PATCH, height // PATCH * (width // PATCH))]
    convert_element_type x3 -> x0, other arithmetic: 8.36 us -> none  [the longest x2 6.21 us: windows(): return halves(x).astype(f32)]
    ppermute x8 -> x0, waiting for transfers between devices: 8 us -> none  [the longest x4 5.33 us: padded_2(): after = lax.ppermute(leading, axis, down)]
    transpose x2 -> x1, local copies, waits for them, and re-layouts: 6.85 us -> 0.1 us  [patch_columns(): x = x.transpose(0, 2, 3, 1, 4)]
    unnamed x40 -> x25, local copies, waits for them, and re-layouts: 9.11 us -> 8.11 us
  transfers between devices with their start and end apart: 8 -> 0, of which waited for: 4 -> 0; matrix products, arithmetic and copies ran while one was open for 6% -> 0% of each run, Pallas kernels for 4% -> 0%
where the time goes in v2:
time: 205 us
  Pallas kernels  175 us (85%)
  local copies, waits for them, and re-layouts  26.5 us (13%)
    pallas_call x1, Pallas kernels, closing(): pl.pallas_call(functools.partial(closing_kernel, tile_rows, tile_cols), o...  72 us
    pallas_call x1, Pallas kernels, per_device(): pl.pallas_call(functools.partial(backward_kernel, tile_rows, tile_cols),...  38.7 us
    pallas_call x1, Pallas kernels, per_device(): pl.pallas_call(functools.partial(forward_kernel, tile_rows, tile_cols), g...  31.1 us
    pallas_call x1, Pallas kernels, mesh_stats(): pl.pallas_call(functools.partial(stats_kernel, rows, cols), out_shape=str...  18.8 us
    pallas_call x1, Pallas kernels, per_device(): pl.pallas_call(functools.partial(embed_kernel, rows, cols, tile_rows, til...  14.4 us
    unnamed x25, local copies, waits for them, and re-layouts  8.11 us

profile of v2, /device:TPU:0, one launch (start us, length us, event | category | flops | bytes accessed | tf_op | source)
XLA Modules:
  0.0 204.6 jit_solution(2971683621288310931)
XLA Ops:
  0.6 0.0 copy-start
  0.6 0.0 copy-start.6
  0.7 0.9 copy-done
  1.6 0.8 reshape.107
  2.4 0.0 copy-start.7
  2.4 0.3 fusion
  2.8 0.1 copy.30
  2.9 0.2 reshape.104
  3.2 0.1 copy.31
  3.3 1.1 reshape.105.patches_ref
  4.3 0.8 broadcast_in_dim.2.w_ref
  5.1 0.0 copy-done.6
  5.1 0.2 copy.34
  5.3 0.0 copy-start.2
  5.3 0.0 copy-done.7
  5.4 0.2 copy.35
  5.6 0.0 copy-start.3
  5.6 1.0 copy.38
  6.6 1.0 copy.37
  7.6 0.2 copy.50
  7.8 0.0 copy-done.2
  7.8 0.0 copy-done.3
  7.9 0.8 copy.33
  8.7 1.3 copy.36.kv_ref
  10.0 14.4 %embed.1.x_ref = f32[2,38,80,128]{3,2,1,0:T(8,128)} custom-call(bf16[48,2048]{1,0:T(8,128)(2,1)} %reshape.105.patches_ref, bf16[48,256]{1,0:T(8,128)(2,1)} %w_ref.1, f32[1,256]{1,0:T(1,128)} %bitcast.107), custom_call_target="tpu_custom_call" | custom-call | tf_op jit(solution)/shard_map/embed/pallas_call | solution.py:557
  24.4 0.0 copy-done.1
  24.4 31.1 %forward.1 = (f32[2,32,64,128]{3,2,1,0:T(8,128)}, bf16[8,2048,256]{2,1,0:T(8,128)(2,1)}, f32[3,8,1,256]{3,2,1,0:T(1,128)}, f32[8,128,256]{2,1,0:T(8,128)}) custom-call(f32[2,38,80,128]{3,2,1,0:T(8,128)} %embed.1.x_ref, f32[2,49,8,128]{3,2,1,0:T(8,128)} %broadcast_in_dim.2.w_ref, f32[1,256]{1,0:T(1,128)} %bitcast.105, bf16[8,256,256]{2,1,0:T(8,128)(2,1)} %copy.36.kv_ref, ...), custom_call_target="tpu_custom_call" | custom-call | tf_op jit(solution)/shard_map/forward/pallas_call | solution.py:584
  55.4 1.3 slice_bitcast_fusion.4.top_ref
  56.7 1.3 copy.67
  58.1 18.8 %stats.1 = f32[2,8,256]{2,1,0:T(8,128)} custom-call(f32[3,8,256]{2,1,0:T(8,128)} %bitcast.100), custom_call_target="tpu_custom_call" | custom-call | tf_op jit(solution)/shard_map/stats/pallas_call | solution.py:515
  76.9 0.7 fusion.9
  77.6 0.6 copy_bitcast_fusion.6
  78.2 38.7 %backward.1 = (bf16[8,2,512,128]{3,2,1,0:T(8,128)(2,1)}, f32[2,32,64,128]{3,2,1,0:T(8,128)}, f32[1,256]{1,0:T(1,128)}) custom-call(f32[2,32,64,128]{3,2,1,0:T(8,128)} %get-tuple-element.16.mixed_ref, f32[1,256]{1,0:T(1,128)} %bitcast.106, bf16[8,2048,256]{2,1,0:T(8,128)(2,1)} %get-tuple-element.17.proj_ref, bf16[8,128,256]{2,1,0:T(8,128)(2,1)} %bitcast.81, ...), custom_call_target="tpu_custom_call" | custom-call | tf_op jit(solution)/shard_map/backward/pallas_call | solution.py:614
  116.9 72.0 %closing.1 = (bf16[8,4,256,128]{3,2,1,0:T(8,128)(2,1)}, f32[8,4,8,128]{3,2,1,0:T(8,128)}) custom-call(bf16[8,4,256,128]{3,2,1,0:T(8,128)(2,1)} %bitcast.90, f32[2,38,80,128]{3,2,1,0:T(8,128)} %embed.1.x_ref, f32[2,32,64,128]{3,2,1,0:T(8,128)} %get-tuple-element.21.d_ref, f32[2,49,8,128]{3,2,1,0:T(8,128)} %broadcast_in_dim.2.w_ref, ...), custom_call_target="tpu_custom_call" | custom-call | tf_op jit(solution)/shard_map/closing/pallas_call | solution.py:454
  188.9 1.3 fusion.8
  190.3 1.4 copy_bitcast_fusion.4
  191.7 0.8 slice.48
  192.6 0.6 copy.54
  193.2 2.0 bitcast_convert_fusion
  195.2 0.1 slice_bitcast_fusion
  195.4 1.5 slice_bitcast_fusion.1
  196.8 1.6 copy.42
  198.4 1.2 copy.64
  199.6 1.2 copy.43
  200.8 0.0 copy-start.4
  200.8 2.2 %copy.63 = f32[32,8,16,128]{3,1,2,0:T(8,128)} copy(f32[32,8,16,128]{3,2,1,0:T(8,128)S(1)} %bitcast.85) | data formatting | bytes 4194304
  203.0 0.4 copy.41
  203.4 1.2 copy.65
  (8 shorter events, 0.1 us)
Async XLA Ops:
  0.6 0.9 copy-start
  0.6 4.5 %copy-start.6 = (bf16[256,1024]{1,0:T(8,128)(2,1)S(1)}, bf16[256,1024]{1,0:T(8,128)(2,1)}, u32[]{:S(2)}) copy-start(bf16[256,1024]{1,0:T(8,128)(2,1)} %param.14) | copy-start | bytes 1572868
  2.4 2.9 %copy-start.7 = (bf16[256,1024]{1,0:T(8,128)(2,1)S(1)}, bf16[256,1024]{1,0:T(8,128)(2,1)}, u32[]{:S(2)}) copy-start(bf16[256,1024]{1,0:T(8,128)(2,1)} %param.15) | copy-start | bytes 1572868
  5.1 2.5 %copy-start.5 = (bf16[256,2048]{1,0:T(8,128)(2,1)S(1)}, bf16[256,2048]{1,0:T(8,128)(2,1)}, u32[]{:S(2)}) copy-start(bf16[256,2048]{1,0:T(8,128)(2,1)} %param.13) | copy-start | bytes 3145732
  5.3 2.5 %copy-start.2 = (bf16[256,1024]{0,1:T(8,128)(2,1)}, bf16[256,1024]{0,1:T(8,128)(2,1)S(1)}, u32[]{:S(2)}) copy-start(bf16[256,1024]{0,1:T(8,128)(2,1)S(1)} %copy.34) | copy-start | bytes 1572868
  5.6 2.3 %copy-start.3 = (bf16[256,1024]{0,1:T(8,128)(2,1)}, bf16[256,1024]{0,1:T(8,128)(2,1)S(1)}, u32[]{:S(2)}) copy-start(bf16[256,1024]{0,1:T(8,128)(2,1)S(1)} %copy.35) | copy-start | bytes 1572868
  8.7 15.7 %copy-start.1 = (bf16[256,2,8,128]{0,3,1,2:T(8,128)(2,1)}, bf16[256,2,8,128]{0,3,1,2:T(8,128)(2,1)S(1)}, u32[]{:S(2)}) copy-start(bf16[256,2,8,128]{0,3,1,2:T(8,128)(2,1)S(1)} %copy.33) | copy-start | bytes 3145732
  200.8 2.2 %copy-start.4 = (f32[2,128,8,128]{1,3,0,2:T(8,128)S(1)}, f32[2,128,8,128]{1,3,0,2:T(8,128)}, u32[]{:S(2)}) copy-start(f32[2,128,8,128]{1,3,0,2:T(8,128)} %get-tuple-element.26) | copy-start | bytes 3145732

commit v3 on v2

--- a/solution.py
+++ b/solution.py
@@ -156,11 +156,10 @@
             normed[rows, :], both, (((0,), (0,)), ((), ())), preferred_element_type=f32
         )
     attended = weighted_ref[0] * jnp.exp2(top_ref[0] - shift)
-    for n in range(large_ref.shape[1]):
-        lanes = slice(n * LANES, (n + 1) * LANES)
-        large_ref[0, n, :LANES] = attended[:, lanes].astype(bf16)
-        large_ref[0, n, LANES : 2 * LANES] = (grad_q[:, lanes] * scale).astype(bf16)
-        large_ref[0, n, 2 * LANES :] = grad_kv[:, lanes].astype(bf16)
+    large_ref[0, 0] = attended.T.astype(bf16)
+    large_ref[0, 1] = (grad_q * scale).T.astype(bf16)
+    large_ref[0, 2] = grad_kv[:, :LANES].astype(bf16)
+    large_ref[0, 3] = grad_kv[:, LANES:].astype(bf16)
 
     @pl.when(pl.program_id(0) == pl.num_programs(0) - 1)
     def _():
@@ -256,11 +255,11 @@
         return buf.at[:, inner, pl.ds(start, 8), :]
 
     def copies():
-        right = pltpu.make_async_remote_copy(
+        right = lambda: pltpu.make_async_remote_copy(
             src_ref=part(tile_cols), dst_ref=part(0), send_sem=sems.at[0, 0], recv_sem=sems.at[1, 0],
             device_id=(row, lax.min(col + 1, cols - 1)), device_id_type=MESH,
         )
-        left = pltpu.make_async_remote_copy(
+        left = lambda: pltpu.make_async_remote_copy(
             src_ref=part(8), dst_ref=part(tile_cols + 8), send_sem=sems.at[0, 1], recv_sem=sems.at[1, 1],
             device_id=(row, lax.max(col - 1, 0)), device_id_type=MESH,
         )
@@ -274,11 +273,11 @@
         return buf.at[:, pl.ds(start, HALF), :, :]
 
     def copies():
-        down = pltpu.make_async_remote_copy(
+        down = lambda: pltpu.make_async_remote_copy(
             src_ref=part(tile_rows), dst_ref=part(0), send_sem=sems.at[0, 2], recv_sem=sems.at[1, 2],
             device_id=(lax.min(row + 1, rows - 1), col), device_id_type=MESH,
         )
-        up = pltpu.make_async_remote_copy(
+        up = lambda: pltpu.make_async_remote_copy(
             src_ref=part(HALF), dst_ref=part(tile_rows + HALF), send_sem=sems.at[0, 3], recv_sem=sems.at[1, 3],
             device_id=(lax.max(row - 1, 0), col), device_id_type=MESH,
         )
@@ -290,55 +289,74 @@
 def run_halo(copies, me, devices):
     @pl.when(me < devices - 1)
     def _():
-        copies()[0].start()
+        copies()[0]().start()
 
     @pl.when(me > 0)
     def _():
-        copies()[1].start()
+        copies()[1]().start()
 
     def wait():
         @pl.when(me > 0)
         def _():
-            copies()[0].wait_recv()
-            copies()[1].wait_send()
+            copies()[0]().wait_recv()
+            copies()[1]().wait_send()
 
         @pl.when(me < devices - 1)
         def _():
-            copies()[1].wait_recv()
-            copies()[0].wait_send()
+            copies()[1]().wait_recv()
+            copies()[0]().wait_send()
 
     return wait
 
 
 class Reduction:
-    def __init__(self, x, out, first, middle, second, sems):
+    def __init__(self, x, out, paired, held, first, middle, second, sems):
         self.x, self.out, self.first, self.middle, self.second = x, out, first, middle, second
+        self.paired, self.held = paired, held
         self.sems = sems
         self.cols, self.rows = x.shape[:2]
         self.row, self.col = lax.axis_index("rows"), lax.axis_index("cols")
+        self.pairs = self.cols // 2
+        self.pair, self.side = self.col // 2, lax.rem(self.col, 2)
+        self.twin = (self.row, self.pair * 2 + 1 - self.side)
         self.copies = []
 
     def across(self, p):
-        return lax.rem(self.col + p, self.cols)
+        return lax.rem(self.pair + p, self.pairs) * 2 + self.side
 
     def along(self, p):
         return lax.rem(self.row + p, self.rows)
 
-    def send_0(self):
-        for p in range(1, self.cols):
-            there = self.across(p)
-            self.copies.append(
-                push(self.x.at[there], self.first.at[p], self.sems, 0, p, (self.row, there))
-            )
-
-    def sum_0(self):
-        for p in range(1, self.cols):
-            source = (self.row, self.across(self.cols - p))
-            await_into(self.first.at[p], self.sems, 0, p, source)
+    def send(self, src, dst, stage, slot, device):
+        self.copies.append(push(src, dst, self.sems, stage, slot, device))
+
+    def send_pair(self):
+        for k in range(self.pairs):
+            self.send(self.x.at[2 * k + 1 - self.side], self.paired.at[k], 0, k, self.twin)
+
+    def sum_pair(self):
+        for k in range(self.pairs):
+            await_into(self.paired.at[k], self.sems, 0, k, self.twin)
+
+        def body(n, carry):
+            k, r = n // self.rows, n % self.rows
+            acc = self.x[2 * k + self.side, r].astype(f32) + self.paired[k, r].astype(f32)
+            self.held[k, r] = acc.astype(self.held.dtype)
+            return carry
+
+        lax.fori_loop(0, self.pairs * self.rows, body, 0)
+        for p in range(1, self.pairs):
+            there = lax.rem(self.pair + p, self.pairs)
+            self.send(self.held.at[there], self.first.at[p], 1, p, (self.row, self.across(p)))
+
+    def sum_cols(self):
+        for p in range(1, self.pairs):
+            source = (self.row, self.across(self.pairs - p))
+            await_into(self.first.at[p], self.sems, 1, p, source)
 
         def body(r, carry):
-            acc = self.x[self.col, r].astype(f32)
-            for p in range(1, self.cols):
+            acc = self.held[self.pair, r].astype(f32)
+            for p in range(1, self.pairs):
                 acc = acc + self.first[p, r].astype(f32)
             self.middle[r] = acc.astype(self.middle.dtype)
             return carry
@@ -346,34 +364,38 @@
         lax.fori_loop(0, self.rows, body, 0)
         for p in range(1, self.rows):
             there = self.along(p)
-            self.copies.append(
-                push(self.middle.at[there], self.second.at[p], self.sems, 1, p, (there, self.col))
-            )
-
-    def sum_1(self):
+            self.send(self.middle.at[there], self.second.at[p], 2, p, (there, self.col))
+
+    def sum_rows(self):
         for p in range(1, self.rows):
             source = (self.along(self.rows - p), self.col)
-            await_into(self.second.at[p], self.sems, 1, p, source)
+            await_into(self.second.at[p], self.sems, 2, p, source)
         acc = self.middle[self.row].astype(f32)
         for p in range(1, self.rows):
             acc = acc + self.second[p].astype(f32)
         self.out[self.col, self.row] = acc.astype(self.out.dtype)
         piece = self.out.at[self.col, self.row]
         for p in range(1, self.rows):
-            self.copies.append(push(piece, piece, self.sems, 2, p, (self.along(p), self.col)))
-
-    def spread_2(self):
+            self.send(piece, piece, 3, p, (self.along(p), self.col))
+
+    def spread_cols(self):
         for p in range(1, self.rows):
             source = self.along(self.rows - p)
-            await_into(self.out.at[self.col, source], self.sems, 2, p, (source, self.col))
+            await_into(self.out.at[self.col, source], self.sems, 3, p, (source, self.col))
         slab = self.out.at[self.col]
-        for p in range(1, self.cols):
-            self.copies.append(push(slab, slab, self.sems, 3, p, (self.row, self.across(p))))
-
-    def spread_3(self):
-        for p in range(1, self.cols):
-            source = self.across(self.cols - p)
-            await_into(self.out.at[source], self.sems, 3, p, (self.row, source))
+        for p in range(1, self.pairs):
+            self.send(slab, slab, 4, p, (self.row, self.across(p)))
+        self.send(slab, slab, 5, 0, self.twin)
+
+    def spread_pair(self):
+        for p in range(1, self.pairs):
+            source = self.across(self.pairs - p)
+            slab = self.out.at[source]
+            await_into(slab, self.sems, 4, p, (self.row, source))
+            self.send(slab, slab, 5, p, self.twin)
+        for p in range(self.pairs):
+            source = lax.rem(self.pair + self.pairs - p, self.pairs) * 2 + 1 - self.side
+            await_into(self.out.at[source], self.sems, 5, p, self.twin)
         for copy in self.copies:
             copy.wait_send()
 
@@ -397,7 +419,8 @@
 def closing_kernel(
     tile_rows, tile_cols, large_ref, x_ref, d_ref, w_ref, patches_ref, gain_ref,
     large_out, small_out,
-    buf, acc, out, flat, small, first, middle, second, s_first, s_middle, s_second,
+    buf, acc, out, flat, small, paired, held, first, middle, second,
+    s_paired, s_held, s_first, s_middle, s_second,
     halo_sems, sems, s_sems,
 ):
     cols, rows = large_ref.shape[:2]
@@ -407,11 +430,12 @@
     buf[:, HALF : HALF + tile_rows, 8 : 8 + tile_cols, :] = d_ref[...]
     flat[...] = jnp.zeros_like(flat)
     greet(row, col, rows, cols)
-    big = Reduction(large_ref, large_out, first, middle, second, sems)
-    little = Reduction(small, small_out, s_first, s_middle, s_second, s_sems)
+    big = Reduction(large_ref, large_out, paired, held, first, middle, second, sems)
+    little = Reduction(small, small_out, s_paired, s_held, s_first, s_middle, s_second, s_sems)
     wait = halo_cols(buf, halo_sems, row, col, cols, tile_rows, tile_cols)
-    big.send_0()
+    big.send_pair()
     kernel_grad(x_ref, d_ref=buf, acc_ref=acc, tile_rows=tile_rows, tile_cols=tile_cols, h=0)
+    big.sum_pair()
     wait()
     wait = halo_rows(buf, halo_sems, row, col, rows, tile_rows)
     kernel_grad(x_ref, d_ref=buf, acc_ref=acc, tile_rows=tile_rows, tile_cols=tile_cols, h=1)
@@ -429,18 +453,19 @@
         flat[base + part - 2 : base + part - 1, :] = jnp.sum(d.astype(f32), axis=0, keepdims=True)
         flat[base + part - 1 : base + part, :] = gain_ref[:, h * LANES : (h + 1) * LANES]
         if h == 0:
-            big.sum_0()
+            big.sum_cols()
     for n in range(cols * rows):
         block = small.shape[2]
         small[n // rows, n % rows] = flat[n * block : (n + 1) * block, :]
-    little.send_0()
-    big.sum_1()
-    little.sum_0()
-    big.spread_2()
-    little.sum_1()
-    little.spread_2()
-    little.spread_3()
-    big.spread_3()
+    little.send_pair()
+    big.sum_rows()
+    little.sum_pair()
+    big.spread_cols()
+    little.sum_cols()
+    little.sum_rows()
+    little.spread_cols()
+    little.spread_pair()
+    big.spread_pair()
 
 
 def closing(large, x, d_mixed, taps_w, patches_t, grad_gain, rows, cols):
@@ -462,15 +487,19 @@
             pltpu.VMEM((2, tile_rows, tile_cols, LANES), f32),
             pltpu.VMEM((pieces * m, LANES), f32),
             pltpu.VMEM((cols, rows, m, LANES), f32),
-            pltpu.VMEM((cols, rows, n, LANES), bf16),
+            pltpu.VMEM((cols // 2, rows, n, LANES), bf16),
+            pltpu.VMEM((cols // 2, rows, n, LANES), bf16),
+            pltpu.VMEM((cols // 2, rows, n, LANES), bf16),
             pltpu.VMEM((rows, n, LANES), bf16),
             pltpu.VMEM((rows, n, LANES), bf16),
-            pltpu.VMEM((cols, rows, m, LANES), f32),
+            pltpu.VMEM((cols // 2, rows, m, LANES), f32),
+            pltpu.VMEM((cols // 2, rows, m, LANES), f32),
+            pltpu.VMEM((cols // 2, rows, m, LANES), f32),
             pltpu.VMEM((rows, m, LANES), f32),
             pltpu.VMEM((rows, m, LANES), f32),
             pltpu.SemaphoreType.DMA((2, 4)),
-            pltpu.SemaphoreType.DMA((2, 4, max(rows, cols))),
-            pltpu.SemaphoreType.DMA((2, 4, max(rows, cols))),
+            pltpu.SemaphoreType.DMA((2, 6, max(rows, cols))),
+            pltpu.SemaphoreType.DMA((2, 6, max(rows, cols))),
         ],
         compiler_params=pltpu.CompilerParams(
             collective_id=2, has_side_effects=True, vmem_limit_bytes=VMEM_LIMIT
@@ -527,6 +556,17 @@
         ),
         name="stats",
     )(x)
+
+
+def format_kernel(large_ref, attended_ref, grad_q_ref, grad_kv_ref):
+    attended_ref[...] = large_ref[0, 0].astype(f32)
+    grad_q_ref[...] = large_ref[0, 1].astype(f32)
+    head = pl.program_id(0)
+    width = grad_kv_ref.shape[1] // 2
+    keys = pl.ds(pl.multiple_of(head * LANES, LANES), LANES)
+    values = pl.ds(pl.multiple_of(width + head * LANES, LANES), LANES)
+    grad_kv_ref[:, keys] = large_ref[0, 2].astype(f32)
+    grad_kv_ref[:, values] = large_ref[0, 3].astype(f32)
 
 
 def head_spec(shape):
@@ -629,12 +669,12 @@
             head_spec((LANES, count)),
         ],
         out_specs=[
-            pl.BlockSpec((1, parts, 4 * LANES, LANES), lambda n: (n, 0, 0, 0)),
+            pl.BlockSpec((1, 4, channels, LANES), lambda n: (n, 0, 0, 0)),
             whole_spec((2, tile_rows, tile_cols, LANES)),
             whole_spec((1, channels)),
         ],
         out_shape=[
-            struct(HEADS, parts, 4 * LANES, LANES, dtype=bf16),
+            struct(HEADS, 4, channels, LANES, dtype=bf16),
             struct(2, tile_rows, tile_cols, LANES),
             struct(1, channels),
         ],
@@ -647,13 +687,23 @@
         name="backward",
     )(mixed, gain, proj, qt, q, dat, da, kvt, shift, dots, tops, weighted)
     large, small = closing(large, x, d_mixed, taps_w, patches_t, grad_gain, rows, cols)
-    large = large.astype(f32).reshape(HEADS, parts, 4 * LANES, LANES)
+    attended, grad_latents, grad_kv = pl.pallas_call(
+        format_kernel,
+        grid=(HEADS,),
+        in_specs=[pl.BlockSpec((1, 4, count, LANES), lambda n: (n, 0, 0, 0))],
+        out_specs=[
+            pl.BlockSpec((count, LANES), lambda n: (0, n)),
+            pl.BlockSpec((count, LANES), lambda n: (0, n)),
+            whole_spec((channels, 2 * model_dim)),
+        ],
+        out_shape=[
+            struct(count, model_dim), struct(count, model_dim), struct(channels, 2 * model_dim)
+        ],
+        name="outputs",
+    )(large.reshape(HEADS, 4, count, LANES))
     half_rows = small.size // (2 * LANES)
     small = small.reshape(2, half_rows, LANES).transpose(1, 0, 2).reshape(half_rows, channels)
     size = patches_t.shape[0]
-    attended = large[:, :, :LANES].transpose(1, 3, 0, 2).reshape(count, model_dim)
-    grad_latents = large[:, :, LANES : 2 * LANES].transpose(1, 3, 0, 2).reshape(count, model_dim)
-    grad_kv = large[:, :, 2 * LANES :].transpose(2, 1, 0, 3).reshape(channels, 2 * model_dim)
     return (
         attended,
         grad_latents,

time: 205 us -> 186 us (0.907)
  local copies, waits for them, and re-layouts: 26.5 us -> 17.1 us
  Pallas kernels: 175 us -> 167 us
    pallas_call x1, Pallas kernels: 72 us -> 57.5 us  [closing(): pl.pallas_call(functools.partial(closing_kernel, tile_rows, tile_cols), o...]
    pallas_call x0 -> x1, Pallas kernels: none -> 6.39 us  [per_device(): pl.pallas_call(format_kernel, grid=(HEADS,), in_specs=[pl.BlockSpec((1, 4...]
    transpose x5 -> x0, local copies, waits for them, and re-layouts: 4.82 us -> none  [the longest x2 3.07 us: per_device(): large[:, :, LANES:2 * LANES].transpose(1, 3, 0, 2).reshape(count, model_dim)]
    unnamed x25 -> x20, local copies, waits for them, and re-layouts: 8.11 us -> 3.57 us
where the time goes in v3:
time: 186 us; the launch traced here: 185 us
  Pallas kernels  167 us (90%)
  local copies, waits for them, and re-layouts  17.1 us (9%)
    pallas_call x1, Pallas kernels, closing(): pl.pallas_call(functools.partial(closing_kernel, tile_rows, tile_cols), o...  57.5 us
    pallas_call x1, Pallas kernels, per_device(): pl.pallas_call(functools.partial(backward_kernel, tile_rows, tile_cols),...  38.7 us
    pallas_call x1, Pallas kernels, per_device(): pl.pallas_call(functools.partial(forward_kernel, tile_rows, tile_cols), g...  31.1 us
    pallas_call x1, Pallas kernels, mesh_stats(): pl.pallas_call(functools.partial(stats_kernel, rows, cols), out_shape=str...  18.8 us
    pallas_call x1, Pallas kernels, per_device(): pl.pallas_call(functools.partial(embed_kernel, rows, cols, tile_rows, til...  14.4 us
    pallas_call x1, Pallas kernels, per_device(): pl.pallas_call(format_kernel, grid=(HEADS,), in_specs=[pl.BlockSpec((1, 4...  6.39 us

profile of v3, /device:TPU:0, one launch (start us, length us, event | category | flops | bytes accessed | tf_op | source)
XLA Modules:
  0.0 185.0 jit_solution(16569076769096494330)
XLA Ops:
  0.6 0.0 copy-start
  0.6 0.0 copy-start.5
  0.7 0.9 copy-done
  1.6 0.8 reshape.89
  2.4 0.0 copy-start.6
  2.4 0.3 fusion
  2.8 0.1 copy.27
  2.9 0.2 reshape.86
  3.2 0.1 copy.28
  3.3 1.1 reshape.87.patches_ref
  4.3 0.8 broadcast_in_dim.2.w_ref
  5.1 0.0 copy-done.5
  5.1 0.0 copy-start.4
  5.1 0.2 copy.31
  5.3 0.0 copy-start.2
  5.3 0.0 copy-done.6
  5.3 0.2 copy.32
  5.6 0.0 copy-start.3
  5.6 1.0 copy.35
  6.6 1.0 copy.34
  7.6 0.0 copy-done.4
  7.6 0.2 copy.44
  7.8 0.0 copy-done.2
  7.8 0.0 copy-done.3
  7.8 0.8 copy.30
  8.6 0.0 copy-start.1
  8.6 1.3 copy.33.kv_ref
  10.0 14.4 %embed.1.x_ref = f32[2,38,80,128]{3,2,1,0:T(8,128)} custom-call(bf16[48,2048]{1,0:T(8,128)(2,1)} %reshape.87.patches_ref, bf16[48,256]{1,0:T(8,128)(2,1)} %w_ref.1, f32[1,256]{1,0:T(1,128)} %bitcast.73), custom_call_target="tpu_custom_call" | custom-call | tf_op jit(solution)/shard_map/embed/pallas_call | solution.py:597
  24.4 0.0 copy-done.1
  24.4 31.1 %forward.1 = (f32[2,32,64,128]{3,2,1,0:T(8,128)}, bf16[8,2048,256]{2,1,0:T(8,128)(2,1)}, f32[3,8,1,256]{3,2,1,0:T(1,128)}, f32[8,128,256]{2,1,0:T(8,128)}) custom-call(f32[2,38,80,128]{3,2,1,0:T(8,128)} %embed.1.x_ref, f32[2,49,8,128]{3,2,1,0:T(8,128)} %broadcast_in_dim.2.w_ref, f32[1,256]{1,0:T(1,128)} %bitcast.71, bf16[8,256,256]{2,1,0:T(8,128)(2,1)} %copy.33.kv_ref, ...), custom_call_target="tpu_custom_call" | custom-call | tf_op jit(solution)/shard_map/forward/pallas_call | solution.py:624
  55.4 1.3 slice_bitcast_fusion.1.top_ref
  56.7 1.3 copy.52
  58.1 18.8 %stats.1 = f32[2,8,256]{2,1,0:T(8,128)} custom-call(f32[3,8,256]{2,1,0:T(8,128)} %bitcast.66), custom_call_target="tpu_custom_call" | custom-call | tf_op jit(solution)/shard_map/stats/pallas_call | solution.py:544
  76.9 0.7 fusion.9
  77.6 0.6 copy_bitcast_fusion.3
  78.2 38.7 %backward.1 = (bf16[8,4,256,128]{3,2,1,0:T(8,128)(2,1)}, f32[2,32,64,128]{3,2,1,0:T(8,128)}, f32[1,256]{1,0:T(1,128)}) custom-call(f32[2,32,64,128]{3,2,1,0:T(8,128)} %get-tuple-element.19.mixed_ref, f32[1,256]{1,0:T(1,128)} %bitcast.72, bf16[8,2048,256]{2,1,0:T(8,128)(2,1)} %get-tuple-element.20.proj_ref, bf16[8,128,256]{2,1,0:T(8,128)(2,1)} %bitcast.55, ...), custom_call_target="tpu_custom_call" | custom-call | tf_op jit(solution)/shard_map/backward/pallas_call | solution.py:654
  116.9 57.5 %closing.1 = (bf16[8,4,256,128]{3,2,1,0:T(8,128)(2,1)}, f32[8,4,8,128]{3,2,1,0:T(8,128)}) custom-call(bf16[8,4,256,128]{3,2,1,0:T(8,128)(2,1)} %get-tuple-element.23.large_ref, f32[2,38,80,128]{3,2,1,0:T(8,128)} %embed.1.x_ref, f32[2,32,64,128]{3,2,1,0:T(8,128)} %get-tuple-element.24.d_ref, f32[2,49,8,128]{3,2,1,0:T(8,128)} %broadcast_in_dim.2.w_ref, ...), custom_call_target="tpu_custom_call" | custom-call | tf_op jit(solution)/shard_map/closing/pallas_call | solution.py:479
  174.4 1.3 fusion.8
  175.7 1.4 copy_bitcast_fusion.1
  177.1 0.8 slice.33
  178.0 0.6 copy.45
  178.6 6.4 %outputs.1 = (f32[256,1024]{1,0:T(8,128)}, f32[256,1024]{1,0:T(8,128)}, f32[256,2048]{1,0:T(8,128)}) custom-call(bf16[8,4,256,128]{3,2,1,0:T(8,128)(2,1)} %get-tuple-element.26.large_ref), custom_call_target="tpu_custom_call" | custom-call | tf_op jit(solution)/shard_map/outputs/pallas_call | solution.py:690
  (4 shorter events, 0.1 us)
Async XLA Ops:
  0.6 0.9 copy-start
  0.6 4.5 %copy-start.5 = (bf16[256,1024]{1,0:T(8,128)(2,1)S(1)}, bf16[256,1024]{1,0:T(8,128)(2,1)}, u32[]{:S(2)}) copy-start(bf16[256,1024]{1,0:T(8,128)(2,1)} %param.14) | copy-start | bytes 1572868
  2.4 2.9 %copy-start.6 = (bf16[256,1024]{1,0:T(8,128)(2,1)S(1)}, bf16[256,1024]{1,0:T(8,128)(2,1)}, u32[]{:S(2)}) copy-start(bf16[256,1024]{1,0:T(8,128)(2,1)} %param.15) | copy-start | bytes 1572868
  5.1 2.5 %copy-start.4 = (bf16[256,2048]{1,0:T(8,128)(2,1)S(1)}, bf16[256,2048]{1,0:T(8,128)(2,1)}, u32[]{:S(2)}) copy-start(bf16[256,2048]{1,0:T(8,128)(2,1)} %param.13) | copy-start | bytes 3145732
  5.3 2.5 %copy-start.2 = (bf16[256,1024]{0,1:T(8,128)(2,1)}, bf16[256,1024]{0,1:T(8,128)(2,1)S(1)}, u32[]{:S(2)}) copy-start(bf16[256,1024]{0,1:T(8,128)(2,1)S(1)} %copy.31) | copy-start | bytes 1572868
  5.6 2.3 %copy-start.3 = (bf16[256,1024]{0,1:T(8,128)(2,1)}, bf16[256,1024]{0,1:T(8,128)(2,1)S(1)}, u32[]{:S(2)}) copy-start(bf16[256,1024]{0,1:T(8,128)(2,1)S(1)} %copy.32) | copy-start | bytes 1572868
  8.6 15.7 %copy-start.1 = (bf16[256,2,8,128]{0,3,1,2:T(8,128)(2,1)}, bf16[256,2,8,128]{0,3,1,2:T(8,128)(2,1)S(1)}, u32[]{:S(2)}) copy-start(bf16[256,2,8,128]{0,3,1,2:T(8,128)(2,1)S(1)} %copy.30) | copy-start | bytes 3145732

commit v4 on v3

--- a/solution.py
+++ b/solution.py
@@ -114,7 +114,7 @@
 
 def backward_kernel(
     tile_rows, tile_cols, mixed_ref, gain_ref, proj_ref, qt_ref, q_ref, dat_ref, da_ref,
-    kvt_ref, shift_ref, dots_ref, top_ref, weighted_ref,
+    kvt_ref, shared_ref, stats_ref, weighted_ref,
     large_ref, d_mixed_ref, grad_gain_ref, normed, d_proj, d_normed,
 ):
     tokens = tile_rows * tile_cols
@@ -133,8 +133,8 @@
 
         lax.fori_loop(0, tile_rows, body, 0)
 
-    shift = shift_ref[0]
-    dots = dots_ref[0]
+    shift = shared_ref[0, 0]
+    dots = shared_ref[1, 0]
     grad_q = jnp.zeros((LANES, shift.shape[1]), f32)
     grad_kv = jnp.zeros((2 * LANES, 2 * LANES), f32)
     for n in range(tokens // chunk):
@@ -155,7 +155,7 @@
         grad_kv = grad_kv + lax.dot_general(
             normed[rows, :], both, (((0,), (0,)), ((), ())), preferred_element_type=f32
         )
-    attended = weighted_ref[0] * jnp.exp2(top_ref[0] - shift)
+    attended = weighted_ref[0] * jnp.exp2(stats_ref[0, 0] - shift)
     large_ref[0, 0] = attended.T.astype(bf16)
     large_ref[0, 1] = (grad_q * scale).T.astype(bf16)
     large_ref[0, 2] = grad_kv[:, :LANES].astype(bf16)
@@ -648,9 +648,7 @@
         compiler_params=params,
         name="forward",
     )(x, taps_w, gain, kv, qt, dat)
-    shared = mesh_stats(stats.reshape(3, HEADS, count), rows, cols)
-    shift, dots = shared.reshape(2, HEADS, 1, count)
-    tops = stats[0]
+    shared = mesh_stats(stats, rows, cols)
     large, d_mixed, grad_gain = pl.pallas_call(
         functools.partial(backward_kernel, tile_rows, tile_cols),
         grid=(HEADS,),
@@ -663,9 +661,8 @@
             head_spec((LANES, count)),
             head_spec((count, LANES)),
             head_spec((2 * LANES, channels)),
-            head_spec((1, count)),
-            head_spec((1, count)),
-            head_spec((1, count)),
+            pl.BlockSpec((2, 1, 1, count), lambda n: (0, n, 0, 0)),
+            pl.BlockSpec((3, 1, 1, count), lambda n: (0, n, 0, 0)),
             head_spec((LANES, count)),
         ],
         out_specs=[
@@ -685,7 +682,7 @@
         ],
         compiler_params=params,
         name="backward",
-    )(mixed, gain, proj, qt, q, dat, da, kvt, shift, dots, tops, weighted)
+    )(mixed, gain, proj, qt, q, dat, da, kvt, shared, stats, weighted)
     large, small = closing(large, x, d_mixed, taps_w, patches_t, grad_gain, rows, cols)
     attended, grad_latents, grad_kv = pl.pallas_call(
         format_kernel,

time: 186 us -> 182 us (0.978)
  local copies, waits for them, and re-layouts: 17.1 us -> 13.1 us
where the time goes in v4:
time: 182 us; the launch traced here: 181 us
  Pallas kernels  167 us (92%)
  local copies, waits for them, and re-layouts  13.1 us (7%)
    pallas_call x1, Pallas kernels, closing(): pl.pallas_call(functools.partial(closing_kernel, tile_rows, tile_cols), o...  57.5 us
    pallas_call x1, Pallas kernels, per_device(): pl.pallas_call(functools.partial(backward_kernel, tile_rows, tile_cols),...  38.6 us
    pallas_call x1, Pallas kernels, per_device(): pl.pallas_call(functools.partial(forward_kernel, tile_rows, tile_cols), g...  31.1 us
    pallas_call x1, Pallas kernels, mesh_stats(): pl.pallas_call(functools.partial(stats_kernel, rows, cols), out_shape=str...  19 us
    pallas_call x1, Pallas kernels, per_device(): pl.pallas_call(functools.partial(embed_kernel, rows, cols, tile_rows, til...  14.4 us
    pallas_call x1, Pallas kernels, per_device(): pl.pallas_call(format_kernel, grid=(HEADS,), in_specs=[pl.BlockSpec((1, 4...  6.39 us

profile of v4, /device:TPU:0, one launch (start us, length us, event | category | flops | bytes accessed | tf_op | source)
XLA Modules:
  0.0 181.3 jit_solution(13737295026320781115)
XLA Ops:
  0.6 0.0 copy-start
  0.6 0.0 copy-start.5
  0.7 0.9 copy-done
  1.6 0.8 reshape.81
  2.4 0.0 copy-start.6
  2.4 0.3 fusion
  2.8 0.1 copy.25
  2.9 0.2 reshape.78
  3.2 0.1 copy.26
  3.3 1.1 reshape.79.patches_ref
  4.3 0.8 broadcast_in_dim.2.w_ref
  5.1 0.0 copy-done.5
  5.1 0.0 copy-start.4
  5.1 0.2 copy.29
  5.3 0.0 copy-start.2
  5.3 0.0 copy-done.6
  5.3 0.2 copy.30
  5.6 0.0 copy-start.3
  5.6 1.0 copy.33
  6.6 1.0 copy.32
  7.6 0.0 copy-done.4
  7.6 0.2 copy.37
  7.8 0.0 copy-done.2
  7.8 0.0 copy-done.3
  7.8 0.8 copy.28
  8.6 0.0 copy-start.1
  8.6 1.3 copy.31.kv_ref
  10.0 14.4 %embed.1.x_ref = f32[2,38,80,128]{3,2,1,0:T(8,128)} custom-call(bf16[48,2048]{1,0:T(8,128)(2,1)} %reshape.79.patches_ref, bf16[48,256]{1,0:T(8,128)(2,1)} %w_ref.1, f32[1,256]{1,0:T(1,128)} %bitcast.63), custom_call_target="tpu_custom_call" | custom-call | tf_op jit(solution)/shard_map/embed/pallas_call | solution.py:597
  24.4 0.0 copy-done.1
  24.4 31.1 %forward.1 = (f32[2,32,64,128]{3,2,1,0:T(8,128)}, bf16[8,2048,256]{2,1,0:T(8,128)(2,1)}, f32[3,8,1,256]{3,2,1,0:T(1,128)}, f32[8,128,256]{2,1,0:T(8,128)}) custom-call(f32[2,38,80,128]{3,2,1,0:T(8,128)} %embed.1.x_ref, f32[2,49,8,128]{3,2,1,0:T(8,128)} %broadcast_in_dim.2.w_ref, f32[1,256]{1,0:T(1,128)} %bitcast.61, bf16[8,256,256]{2,1,0:T(8,128)(2,1)} %copy.31.kv_ref, ...), custom_call_target="tpu_custom_call" | custom-call | tf_op jit(solution)/shard_map/forward/pallas_call | solution.py:624
  55.4 19.0 %stats.1.shared_ref = f32[2,8,1,256]{3,2,1,0:T(1,128)} custom-call(f32[3,8,1,256]{3,2,1,0:T(1,128)} %get-tuple-element.21.x_ref.stats_ref), custom_call_target="tpu_custom_call" | custom-call | tf_op jit(solution)/shard_map/stats/pallas_call | solution.py:544
  74.4 38.6 %backward.1 = (bf16[8,4,256,128]{3,2,1,0:T(8,128)(2,1)}, f32[2,32,64,128]{3,2,1,0:T(8,128)}, f32[1,256]{1,0:T(1,128)}) custom-call(f32[2,32,64,128]{3,2,1,0:T(8,128)} %get-tuple-element.19.mixed_ref, f32[1,256]{1,0:T(1,128)} %bitcast.62, bf16[8,2048,256]{2,1,0:T(8,128)(2,1)} %get-tuple-element.20.proj_ref, bf16[8,128,256]{2,1,0:T(8,128)(2,1)} %bitcast.46, ...), custom_call_target="tpu_custom_call" | custom-call | tf_op jit(solution)/shard_map/backward/pallas_call | solution.py:652
  113.1 57.5 %closing.1 = (bf16[8,4,256,128]{3,2,1,0:T(8,128)(2,1)}, f32[8,4,8,128]{3,2,1,0:T(8,128)}) custom-call(bf16[8,4,256,128]{3,2,1,0:T(8,128)(2,1)} %get-tuple-element.23.large_ref, f32[2,38,80,128]{3,2,1,0:T(8,128)} %embed.1.x_ref, f32[2,32,64,128]{3,2,1,0:T(8,128)} %get-tuple-element.24.d_ref, f32[2,49,8,128]{3,2,1,0:T(8,128)} %broadcast_in_dim.2.w_ref, ...), custom_call_target="tpu_custom_call" | custom-call | tf_op jit(solution)/shard_map/closing/pallas_call | solution.py:479
  170.6 1.3 fusion.8
  171.9 1.4 copy_bitcast_fusion.1
  173.4 0.8 slice.27
  174.2 0.6 copy.38
  174.9 6.4 %outputs.1 = (f32[256,1024]{1,0:T(8,128)}, f32[256,1024]{1,0:T(8,128)}, f32[256,2048]{1,0:T(8,128)}) custom-call(bf16[8,4,256,128]{3,2,1,0:T(8,128)(2,1)} %get-tuple-element.26.large_ref), custom_call_target="tpu_custom_call" | custom-call | tf_op jit(solution)/shard_map/outputs/pallas_call | solution.py:687
  (4 shorter events, 0.1 us)
Async XLA Ops:
  0.6 0.9 copy-start
  0.6 4.5 %copy-start.5 = (bf16[256,1024]{1,0:T(8,128)(2,1)S(1)}, bf16[256,1024]{1,0:T(8,128)(2,1)}, u32[]{:S(2)}) copy-start(bf16[256,1024]{1,0:T(8,128)(2,1)} %param.14) | copy-start | bytes 1572868
  2.4 2.9 %copy-start.6 = (bf16[256,1024]{1,0:T(8,128)(2,1)S(1)}, bf16[256,1024]{1,0:T(8,128)(2,1)}, u32[]{:S(2)}) copy-start(bf16[256,1024]{1,0:T(8,128)(2,1)} %param.15) | copy-start | bytes 1572868
  5.1 2.5 %copy-start.4 = (bf16[256,2048]{1,0:T(8,128)(2,1)S(1)}, bf16[256,2048]{1,0:T(8,128)(2,1)}, u32[]{:S(2)}) copy-start(bf16[256,2048]{1,0:T(8,128)(2,1)} %param.13) | copy-start | bytes 3145732
  5.3 2.5 %copy-start.2 = (bf16[256,1024]{0,1:T(8,128)(2,1)}, bf16[256,1024]{0,1:T(8,128)(2,1)S(1)}, u32[]{:S(2)}) copy-start(bf16[256,1024]{0,1:T(8,128)(2,1)S(1)} %copy.29) | copy-start | bytes 1572868
  5.6 2.3 %copy-start.3 = (bf16[256,1024]{0,1:T(8,128)(2,1)}, bf16[256,1024]{0,1:T(8,128)(2,1)S(1)}, u32[]{:S(2)}) copy-start(bf16[256,1024]{0,1:T(8,128)(2,1)S(1)} %copy.30) | copy-start | bytes 1572868
  8.6 15.7 %copy-start.1 = (bf16[256,2,8,128]{0,3,1,2:T(8,128)(2,1)}, bf16[256,2,8,128]{0,3,1,2:T(8,128)(2,1)S(1)}, u32[]{:S(2)}) copy-start(bf16[256,2,8,128]{0,3,1,2:T(8,128)(2,1)S(1)} %copy.28) | copy-start | bytes 3145732
